TPU v7x, 32 devices: a whole 2x2x4 slice. The times are simulated.
32 devices in a mesh: row: 4 (over y, x), col: 8 (over z, core).
Axes of the slice: x: 2, y: 2, z: 4, core: 2. Of those that a mesh axis runs over, the one named last changes fastest.
Arguments:
- playlist_items: bfloat16 [4096, 8192], P('row', 'col'), may hold values from -6 to 6
- tile_live: int32 [4, 8], P('row', 'col'), may hold values 0 or 1
- playlist_weights: int32 [4096], P('row'), may hold values from 1 to 8
Outputs:
- cooccur: float32 [4096, 8192], P('row', 'col')
All inputs are finite; a program needn't handle non-finite values. No bound on the sum of `tile_live` on one device may be relied on, other than what follows from the above.
Results may differ from a plain program's by a relative error of at most 0.002.
Values may be sent and summed in bfloat16 or wider, within the bound.
No kernel may reach another device: no remote copies, remote signals or barrier semaphores. Data moves between devices by JAX's collectives and lax.ppermute only.
A program may use at most 128 MiB of HBM per device.

v0:
```python
import jax
import jax.numpy as jnp
from jax import lax
from jax.sharding import PartitionSpec as P


def broadcast(x, axis, root):
    mine = lax.axis_index(axis) == root
    return lax.psum(jnp.where(mine, x, jnp.zeros_like(x)), axis)


def per_device(playlist_items, tile_live, playlist_weights):
    masked = jnp.where(tile_live[0, 0] > 0, playlist_items, jnp.zeros_like(playlist_items))
    whole_column, weights_all = (
        lax.all_gather(masked, "row", axis=0, tiled=True),
        lax.all_gather(playlist_weights, "row", axis=0, tiled=True),
    )
    scaled = (weights_all[:, None].astype(jnp.float32) * whole_column.astype(jnp.float32)).astype(
        jnp.bfloat16
    )
    total_rows = whole_column.shape[0]
    owner_index = lax.axis_index("row")
    band_block = broadcast(whole_column, "col", owner_index)
    summed = lax.dot_general(
        band_block, scaled, (((0,), (0,)), ((), ())), preferred_element_type=jnp.float32
    )
    return summed / jnp.float32(total_rows)


def solution(mesh):
    return jax.shard_map(
        per_device,
        mesh=mesh,
        in_specs=(P("row", "col"), P("row", "col"), P("row")),
        out_specs=P("row", "col"),
        check_vma=False,
    )
```

profile of v0, /device:TPU:30, one launch (start us, length us, event | category | flops | bytes accessed | tf_op | source)
XLA Modules:
  0.0 301.3 jit_solution(17383037097966673358)
XLA Ops:
  6.5 0.0 all-gather.2.cloned.1.call-start
  7.2 3.1 %broadcast_select_fusion.1 = bf16[1024,1024]{1,0:T(8,128)(2,1)} fusion(bf16[1024,1024]{1,0:T(8,128)(2,1)} %param.3, pred[]{:T(512)} %bitcast), kind=kLoop, calls=%fused_computation.5 | loop fusion | flops 1048576 | bytes 4194305 | tf_op jit(solution)/shard_map/jit(_where)/select_n | solution.py:13
  10.2 0.0 all-gather.2.cloned.1.call-update
  10.3 0.0 all-reduce.2.cloned.1.call-start
  10.3 87.7 %all-gather.2.cloned.1.call-done = bf16[4096,1024]{1,0:T(8,128)(2,1)} async-done(((bf16[1024,1024]{1,0:T(8,128)(2,1)}), bf16[4096,1024]{1,0:T(8,128)(2,1)}) %all-gather.2.cloned.1.call-update) | async-done | bytes 8388624 | tf_op jit(solution)/shard_map/all_gather | solution.py:15
  98.0 3.8 %broadcast_select_fusion = bf16[4096,1024]{1,0:T(8,128)(2,1)} fusion(bf16[4096,1024]{1,0:T(8,128)(2,1)} %all-gather.2.cloned.1.call-done, pred[]{:T(512)S(6)} %eq.3), kind=kLoop, calls=%fused_computation.3 | loop fusion | flops 4194304 | bytes 16777216 | tf_op jit(solution)/shard_map/jit(_where)/select_n | solution.py:9
  101.8 0.0 copy-start
  101.8 0.0 all-reduce.2.cloned.1.call-update
  101.8 0.7 copy-done
  102.5 8.1 %all_gather.7 = s32[4096]{0:T(1024)S(1)} all-gather(s32[1024]{0:T(1024)S(1)} %copy-done), channel_id=1, replica_groups=mesh['row'=4,'col'=8] {'row'}, dimensions={0}, use_global_device_ids=true | all-gather | bytes 20480 | tf_op jit(solution)/shard_map/all_gather | solution.py:16
  110.6 168.6 %all-reduce.2.cloned.1.call-done = bf16[4096,1024]{1,0:T(8,128)(2,1)} async-done(((bf16[4096,1024]{1,0:T(8,128)(2,1)}), bf16[4096,1024]{1,0:T(8,128)(2,1)}) %all-reduce.2.cloned.1.call-update) | async-done | bytes 8388624 | tf_op jit(solution)/shard_map/psum | solution.py:9
  279.2 15.3 %fusion.2 = f32[1024,1024]{1,0:T(8,128)} fusion(bf16[4096,1024]{1,0:T(8,128)(2,1)} %all-reduce.2.cloned.1.call-done, bf16[4096,1024]{1,0:T(8,128)(2,1)} %all-gather.2.cloned.1.call-done, f32[4096]{0:T(1024)S(1)} %convert_element_type.10), kind=kOutput, calls=%fused_computation.4 | convolution fusion | flops 8603566080 | bytes 20987904 | tf_op jit(solution)/shard_map/dot_general | solution.py:24
  (1 shorter events, 0.0 us)
Async XLA Ops:
  6.5 91.5 %all-gather.2.cloned.1.call-start = ((), (), s32[]{:S(2)}) async-start(), calls=%async_computation | async-start | bytes 10485760 | tf_op jit(solution)/shard_map/all_gather | solution.py:15
  10.3 268.9 %all-reduce.2.cloned.1.call-start = ((), (), s32[]{:S(2)}) async-start(), calls=%async_computation.1 | async-start | bytes 16777216 | tf_op jit(solution)/shard_map/psum | solution.py:9
  101.8 0.7 copy-start
Sparse Core Ops, SparseCore 0:
  10.4 87.5 all-gather.1
  101.9 177.2 all-reduce.1
where the time goes:
time: 304 us; the launch traced here: 301 us
  waiting for transfers between devices  256 us (84%)
  matrix products  15.3 us (5%)
  between operations  14.1 us (5%)
  blocking collectives  8.11 us (3%)
  other arithmetic  6.82 us (2%)
    psum x1, waiting for transfers between devices, broadcast(): return lax.psum(jnp.where(mine, x, jnp.zeros_like(x)), axis)  169 us
    all_gather x1, waiting for transfers between devices, per_device(): lax.all_gather(masked, 'row', axis=0, tiled=True)  87.7 us
    dot_general x1, matrix products, per_device(): lax.dot_general(band_block, scaled, (((0,), (0,)), ((), ())), preferred_e...  15.3 us
    all_gather x1, blocking collectives, per_device(): lax.all_gather(playlist_weights, 'row', axis=0, tiled=True)  8.11 us
  transfers between devices with their start and end apart: 2, of which 2 were waited for; matrix products, arithmetic and copies ran while one was open for 0% of the time, Pallas kernels for 0%

commit v1 on v0

v1 whole, which is shorter than its diff:
```python
import jax
import jax.numpy as jnp
from jax import lax
from jax.sharding import PartitionSpec as P


def broadcast(x, axis, root):
    mine = lax.axis_index(axis) == root
    return lax.psum(jnp.where(mine, x, jnp.zeros_like(x)), axis)


def per_device_general(playlist_items, tile_live, playlist_weights):
    masked = jnp.where(tile_live[0, 0] > 0, playlist_items, jnp.zeros_like(playlist_items))
    column = lax.all_gather(masked, "row", axis=0, tiled=True)
    weights = lax.all_gather(playlist_weights, "row", axis=0, tiled=True)
    scaled = (weights[:, None].astype(jnp.float32) * column.astype(jnp.float32)).astype(jnp.bfloat16)
    band = broadcast(column, "col", lax.axis_index("row"))
    summed = lax.dot_general(band, scaled, (((0,), (0,)), ((), ())), preferred_element_type=jnp.float32)
    return summed / jnp.float32(column.shape[0])


def pairs(*rules):
    out = []
    for n in range(32):
        at = (n >> 4, (n >> 3) & 1, (n >> 1) & 3, n & 1)
        for rule in rules:
            to = rule(*at)
            if to is not None:
                out.append((n, to[0] * 16 + to[1] * 8 + to[2] * 2 + to[3]))
    return out


def across(y, x, z, k):
    return (y, k, z, x) if z < 2 else None


def one_up(y, x, z, k):
    return (y, x, z + 1, k) if z < 2 else None


def one_to_two(y, x, z, k):
    return (y, x, 2, k) if z == 1 else None


def two_to_three(y, x, z, k):
    return (y, x, 3, k) if z == 2 else None


def one_to_none(y, x, z, k):
    return (y, x, 0, k) if z == 1 else None


ACROSS, ONE_UP, ONE_TO_TWO = pairs(across), pairs(one_up), pairs(one_to_two)
OUTWARD, TWO_TO_THREE = pairs(two_to_three, one_to_none), pairs(two_to_three)
SWAP_X = pairs(lambda y, x, z, k: (y, 1 - x, z, k))
SWAP_Y = pairs(lambda y, x, z, k: (1 - y, x, z, k))
SWAP_Z = pairs(lambda y, x, z, k: (y, x, z ^ 1, k))
CORES = pairs(lambda y, x, z, k: (y, x, z, 1 - k))


def send(value, perm):
    return lax.ppermute(value, ("row", "col"), perm)


def after(value, *others):
    return lax.optimization_barrier((value,) + others)[0]


def cuts_of(cols):
    unit = cols // 8
    at, out = 0, []
    for width in (1, 3, 3, 1):
        out.append((at, at + width * unit))
        at += width * unit
    return out


def per_device(playlist_items, tile_live, playlist_weights):
    rows, cols = playlist_items.shape
    r, c = lax.axis_index("row"), lax.axis_index("col")
    y, x, z, k = r // 2, r % 2, c // 2, c % 2
    live = tile_live[0, 0] > 0
    cuts = cuts_of(cols)

    def keep(block):
        return jnp.where(live, block, jnp.zeros_like(block))

    n = len(cuts)
    pieces = [keep(playlist_items[:, lo:hi]) for lo, hi in cuts]
    own = keep(playlist_items)
    w_near = send(playlist_weights, SWAP_X)
    base, up, up2, out, out2 = [], [], [], [], []
    for j in range(n):
        base.append(send(after(pieces[j], base[j - 2]) if j >= 2 else after(pieces[j], w_near), ACROSS))
    near = send(after(own, w_near, *base), SWAP_X)
    for j in range(n):
        up.append(send(after(base[j], up[j - 1]) if j >= 2 else base[j], ONE_UP))
        up2.append(send(after(up[j], up2[j - 1]) if j >= 1 else up[j], ONE_TO_TWO))
        out.append(send(jnp.where(z == 1, base[j], up[j]), OUTWARD))
        out2.append(send(up2[j], TWO_TO_THREE))

    def scale(block, weight):
        return (weight[:, None].astype(jnp.float32) * block.astype(jnp.float32)).astype(jnp.bfloat16)

    def dot(lhs, rhs):
        return lax.dot_general(lhs, rhs, (((0,), (0,)), ((), ())), preferred_element_type=jnp.float32)

    here, there = scale(own, playlist_weights), scale(near, w_near)
    by_mine, by_their = jnp.where(k == x, here, there), jnp.where(k == x, there, here)
    outs, fars = [], []
    for j, (lo, hi) in enumerate(cuts):
        high = jnp.where(z == 1, base[j], jnp.where(z == 2, up[j], out[j]))
        low = jnp.where(z == 0, base[j], jnp.where(z == 1, up[j], up2[j] + out2[j]))
        mine = jnp.concatenate([jnp.where(y == 1, high, low), jnp.where(y == 1, low, high)], 1)
        if j >= 2:
            mine = after(mine, fars[j - 2])
        their = send(mine, CORES)
        part = dot(mine, by_mine) + dot(their, by_their)
        far = send(part[hi - lo :].astype(jnp.bfloat16), SWAP_Y)
        fars.append(far)
        outs.append((part[: hi - lo] + far.astype(jnp.float32)) / jnp.float32(4 * rows))
    return jnp.concatenate(outs, 0)


def solution(mesh):
    tuned = mesh.shape["row"] == 4 and mesh.shape["col"] == 8
    return jax.shard_map(
        per_device if tuned else per_device_general,
        mesh=mesh,
        in_specs=(P("row", "col"), P("row", "col"), P("row")),
        out_specs=P("row", "col"),
        check_vma=False,
    )
```

time: 304 us -> 189 us (0.62)
  waiting for transfers between devices: 256 us -> 134 us
  starting transfers between devices: 0.04 us -> 26.5 us
  between operations: 14.1 us -> 1.29 us
  blocking collectives: 8.11 us -> 0 us
  other arithmetic: 6.82 us -> 13.2 us
  matrix products: 15.3 us -> 10.4 us
    psum x1 -> x0, waiting for transfers between devices: 169 us -> none  [broadcast(): return lax.psum(jnp.where(mine, x, jnp.zeros_like(x)), axis)]
    ppermute x0 -> x30, waiting for transfers between devices: none -> 134 us  [send(): return lax.ppermute(value, ('row', 'col'), perm)]
    all_gather x1 -> x0, waiting for transfers between devices: 87.7 us -> none  [per_device(): lax.all_gather(masked, 'row', axis=0, tiled=True)]
    ppermute x0 -> x30, starting transfers between devices: none -> 26.5 us  [send(): return lax.ppermute(value, ('row', 'col'), perm)]
    all_gather x1 -> x0, blocking collectives: 8.11 us -> none  [per_device(): lax.all_gather(playlist_weights, 'row', axis=0, tiled=True)]
    dot_general x1 -> x8, matrix products: 15.3 us -> 10.4 us  [dot(): lax.dot_general(lhs, rhs, (((0,), (0,)), ((), ())), preferred_element_typ...]
    select_n x2 -> x16, other arithmetic: 6.81 us -> 9.59 us  [the longest x3 3.31 us: keep(): return jnp.where(live, block, jnp.zeros_like(block))]
  transfers between devices with their start and end apart: 2 -> 30, of which waited for: 2 -> 9; matrix products, arithmetic and copies ran while one was open for 0% -> 11% of each run, Pallas kernels for 0% -> 0%
where the time goes in v1:
time: 189 us; the launch traced here: 186 us
  waiting for transfers between devices  134 us (71%)
  starting transfers between devices  26.5 us (14%)
  other arithmetic  13.2 us (7%)
  matrix products  10.4 us (6%)
    ppermute x30, waiting for transfers between devices, send(): return lax.ppermute(value, ('row', 'col'), perm)  134 us
    ppermute x30, starting transfers between devices, send(): return lax.ppermute(value, ('row', 'col'), perm)  26.5 us
    dot_general x8, matrix products, dot(): lax.dot_general(lhs, rhs, (((0,), (0,)), ((), ())), preferred_element_typ...  10.4 us
  transfers between devices with their start and end apart: 30, of which 9 were waited for; matrix products, arithmetic and copies ran while one was open for 11% of the time, Pallas kernels for 0%

profile of v1, /device:TPU:30, one launch (start us, length us, event | category | flops | bytes accessed | tf_op | source)
XLA Modules:
  0.0 186.1 jit_solution(6785457440962993444)
XLA Ops:
  1.3 2.4 %slice_select_fusion = (bf16[1024,384]{1,0:T(8,128)(2,1)}, bf16[1024,384]{1,0:T(8,128)(2,1)S(1)}) fusion(bf16[1024,1024]{1,0:T(8,128)(2,1)} %param.3, pred[]{:T(512)} %bitcast), kind=kLoop, calls=%fused_computation.22 | loop fusion | flops 786432 | bytes 3145729 | tf_op jit(solution)/shard_map/jit(_where)/select_n | solution.py:86
  3.8 1.5 collective-permute-start.6
  6.8 1.6 collective-permute-start.12
  9.8 1.4 collective-permute-start.4
  15.4 1.3 collective-permute-start.9
  17.5 26.3 %collective-permute-done.3 = bf16[1024,128]{1,0:T(8,128)(2,1)S(1)} collective-permute-done((bf16[1024,128]{1,0:T(8,128)(2,1)S(1)}, bf16[1024,128]{1,0:T(8,128)(2,1)S(1)}, u32[]{:S(2)}, u32[]{:S(2)}) %collective-permute-start.3) | collective-permute-done | bytes 262176 | tf_op jit(solution)/shard_map/ppermute | solution.py:62
  43.8 10.0 %collective-permute-done.5 = bf16[1024,128]{1,0:T(8,128)(2,1)S(1)} collective-permute-done((bf16[1024,128]{1,0:T(8,128)(2,1)}, bf16[1024,128]{1,0:T(8,128)(2,1)S(1)}, u32[]{:S(2)}, u32[]{:S(2)}) %collective-permute-start.5) | collective-permute-done | bytes 262176 | tf_op jit(solution)/shard_map/ppermute | solution.py:62
  56.1 1.3 collective-permute-start.13
  61.1 17.4 %collective-permute-done.13 = bf16[1024,384]{1,0:T(8,128)(2,1)S(1)} collective-permute-done((bf16[1024,384]{1,0:T(8,128)(2,1)S(1)}, bf16[1024,384]{1,0:T(8,128)(2,1)S(1)}, u32[]{:S(2)}, u32[]{:S(2)}) %collective-permute-start.13) | collective-permute-done | bytes 786464 | tf_op jit(solution)/shard_map/ppermute | solution.py:62
  79.2 13.4 %collective-permute-done.15 = bf16[1024,384]{1,0:T(8,128)(2,1)S(1)} collective-permute-done((bf16[1024,384]{1,0:T(8,128)(2,1)S(1)}, bf16[1024,384]{1,0:T(8,128)(2,1)S(1)}, u32[]{:S(2)}, u32[]{:S(2)}) %collective-permute-start.15) | collective-permute-done | bytes 786464 | tf_op jit(solution)/shard_map/ppermute | solution.py:62
  93.9 1.7 broadcast_select_fusion.8
  95.9 1.3 collective-permute-start.21
  97.2 1.4 broadcast_select_fusion.2
  100.8 7.8 %collective-permute-done.19 = bf16[1024,384]{1,0:T(8,128)(2,1)S(1)} collective-permute-done((bf16[1024,384]{1,0:T(8,128)(2,1)S(1)}, bf16[1024,384]{1,0:T(8,128)(2,1)S(1)}, u32[]{:S(2)}, u32[]{:S(2)}) %collective-permute-start.19) | collective-permute-done | bytes 786464 | tf_op jit(solution)/shard_map/ppermute | solution.py:62
  109.1 1.5 collective-permute-start.27
  110.6 18.4 %collective-permute-done.21 = bf16[1024,384]{1,0:T(8,128)(2,1)S(1)} collective-permute-done((bf16[1024,384]{1,0:T(8,128)(2,1)S(1)}, bf16[1024,384]{1,0:T(8,128)(2,1)S(1)}, u32[]{:S(2)}, u32[]{:S(2)}) %collective-permute-start.21) | collective-permute-done | bytes 786464 | tf_op jit(solution)/shard_map/ppermute | solution.py:62
  129.7 1.8 fusion.5
  131.5 1.9 %convolution_add_fusion.1 = f32[768,1024]{1,0:T(8,128)S(1)} fusion(f32[768,1024]{1,0:T(8,128)S(1)} %fusion.5, bf16[1024,1024]{1,0:T(8,128)(2,1)S(1)} %get-tuple-element.41, bf16[1024,384]{1,0:T(8,128)(2,1)S(1)} %broadcast_select_fusion.7, bf16[1024,384]{1,0:T(8,128)(2,1)S(1)} %get-tuple-element.35), kind=kOutput, calls=%fused_computation.7 | convolution fusion | flops 1614544896 | bytes 9961472 | tf_op jit(solution)/shard_map/dot_general | solution.py:106
  134.4 19.1 %collective-permute-done.17 = bf16[384,1024]{1,0:T(8,128)(2,1)S(1)} collective-permute-done((bf16[384,1024]{1,0:T(8,128)(2,1)S(1)}, bf16[384,1024]{1,0:T(8,128)(2,1)S(1)}, u32[]{:S(2)}, u32[]{:S(2)}) %collective-permute-start.17) | collective-permute-done | bytes 786464 | tf_op jit(solution)/shard_map/ppermute | solution.py:62
  153.5 1.8 fusion.6
  155.4 2.0 %convolution_add_fusion = f32[768,1024]{1,0:T(8,128)S(1)} fusion(f32[768,1024]{1,0:T(8,128)S(1)} %fusion.6, bf16[1024,768]{1,0:T(8,128)(2,1)S(1)} %pad_maximum_fusion.2, bf16[1024,1024]{1,0:T(8,128)(2,1)S(1)} %get-tuple-element.41), kind=kOutput, calls=%fused_computation.6 | convolution fusion | flops 1611399168 | bytes 9961472 | tf_op jit(solution)/shard_map/dot_general | solution.py:106
  159.6 1.6 collective-permute-start.29
  161.4 21.7 %collective-permute-done.29 = bf16[128,1024]{1,0:T(8,128)(2,1)S(1)} collective-permute-done((bf16[128,1024]{1,0:T(8,128)(2,1)S(1)}, bf16[128,1024]{1,0:T(8,128)(2,1)S(1)}, u32[]{:S(2)}, u32[]{:S(2)}) %collective-permute-start.29) | collective-permute-done | bytes 262176 | tf_op jit(solution)/shard_map/ppermute | solution.py:62
  183.5 2.6 %pad_maximum_fusion = f32[1024,1024]{1,0:T(8,128)} fusion(f32[128,1024]{1,0:T(8,128)S(1)} %fusion.2, f32[384,1024]{1,0:T(8,128)S(1)} %fusion, f32[384,1024]{1,0:T(8,128)S(1)} %fusion.1, f32[128,1024]{1,0:T(8,128)S(1)} %fusion.3), kind=kLoop, calls=%fused_computation | loop fusion | flops 3145728 | bytes 8388608 | tf_op jit(solution)/shard_map/concatenate | solution.py:122
  (79 shorter events, 23.5 us)
Async XLA Ops:
  0.0 3.8 %collective-permute-start = (s32[1024]{0:T(1024)}, s32[1024]{0:T(1024)S(1)}, u32[]{:S(2)}, u32[]{:S(2)}) collective-permute-start(s32[1024]{0:T(1024)} %param.5), channel_id=1, source_target_pairs={{0,8},{1,9},{2,10},{3,11},{4,12},{5,13},{6,14},{7,15},{8,0},{9,1},... | collective-permute-start | bytes 12296 | tf_op jit(solution)/shard_map/ppermute | solution.py:62
  6.8 7.7 %collective-permute-start.12 = (bf16[1024,384]{1,0:T(8,128)(2,1)}, bf16[1024,384]{1,0:T(8,128)(2,1)}, u32[]{:S(2)}, u32[]{:S(2)}) collective-permute-start(bf16[1024,384]{1,0:T(8,128)(2,1)} %collective-permute-done.6), channel_id=1, source_target_pairs={{0,2},{1,3},{2,4},{3,5},{8,10},{9,11},{10,12},{11,13},{16,18},{17,... | collective-permute-start | bytes 2359304 | tf_op jit(solution)/shard_map/ppermute | solution.py:62
  9.1 6.3 %collective-permute-start.7 = (bf16[1024,384]{1,0:T(8,128)(2,1)}, bf16[1024,384]{1,0:T(8,128)(2,1)S(1)}, u32[]{:S(2)}, u32[]{:S(2)}) collective-permute-start(bf16[1024,384]{1,0:T(8,128)(2,1)} %get-tuple-element.19), channel_id=1, source_target_pairs={{0,0},{1,8},{2,2},{3,10},{8,1},{9,9},{10,3},{11,11},{16,16},{17,24... | collective-permute-start | bytes 2359304 | tf_op jit(solution)/shard_map/ppermute | solution.py:62
  11.2 32.5 %collective-permute-start.3 = (bf16[1024,128]{1,0:T(8,128)(2,1)S(1)}, bf16[1024,128]{1,0:T(8,128)(2,1)S(1)}, u32[]{:S(2)}, u32[]{:S(2)}) collective-permute-start(bf16[1024,128]{1,0:T(8,128)(2,1)S(1)} %broadcast_select_fusion.10), channel_id=1, source_target_pairs={{2,0},{3,1},{4,6},{5,7},{10,8},{11,9},{12,14},{13,15},{18,16},{19,... | collective-permute-start | bytes 786440 | tf_op jit(solution)/shard_map/ppermute | solution.py:62
  13.2 40.6 %collective-permute-start.5 = (bf16[1024,128]{1,0:T(8,128)(2,1)}, bf16[1024,128]{1,0:T(8,128)(2,1)S(1)}, u32[]{:S(2)}, u32[]{:S(2)}) collective-permute-start(bf16[1024,128]{1,0:T(8,128)(2,1)} %collective-permute-done.4), channel_id=1, source_target_pairs={{4,6},{5,7},{12,14},{13,15},{20,22},{21,23},{28,30},{29,31}} | collective-permute-start | bytes 786440 | tf_op jit(solution)/shard_map/ppermute | solution.py:62
  14.5 42.8 %collective-permute-start.14 = (bf16[1024,384]{1,0:T(8,128)(2,1)}, bf16[1024,384]{1,0:T(8,128)(2,1)S(1)}, u32[]{:S(2)}, u32[]{:S(2)}) collective-permute-start(bf16[1024,384]{1,0:T(8,128)(2,1)} %collective-permute-done.12), channel_id=1, source_target_pairs={{2,4},{3,5},{10,12},{11,13},{18,20},{19,21},{26,28},{27,29}} | collective-permute-start | bytes 2359304 | tf_op jit(solution)/shard_map/ppermute | solution.py:62
  15.4 80.5 %collective-permute-start.9 = (bf16[1024,1024]{1,0:T(8,128)(2,1)S(1)}, bf16[1024,1024]{1,0:T(8,128)(2,1)S(1)}, u32[]{:S(2)}, u32[]{:S(2)}) collective-permute-start(bf16[1024,1024]{1,0:T(8,128)(2,1)S(1)} %broadcast_select_fusion), channel_id=1, source_target_pairs={{0,8},{1,9},{2,10},{3,11},{4,12},{5,13},{6,14},{7,15},{8,0},{9,1},... | collective-permute-start | bytes 6291464 | tf_op jit(solution)/shard_map/ppermute | solution.py:62
  16.8 42.1 %collective-permute-start.18 = (bf16[1024,384]{1,0:T(8,128)(2,1)S(1)}, bf16[1024,384]{1,0:T(8,128)(2,1)S(1)}, u32[]{:S(2)}, u32[]{:S(2)}) collective-permute-start(bf16[1024,384]{1,0:T(8,128)(2,1)S(1)} %collective-permute-done.7), channel_id=1, source_target_pairs={{0,2},{1,3},{2,4},{3,5},{8,10},{9,11},{10,12},{11,13},{16,18},{17,... | collective-permute-start | bytes 2359304 | tf_op jit(solution)/shard_map/ppermute | solution.py:62
  56.1 22.4 %collective-permute-start.13 = (bf16[1024,384]{1,0:T(8,128)(2,1)S(1)}, bf16[1024,384]{1,0:T(8,128)(2,1)S(1)}, u32[]{:S(2)}, u32[]{:S(2)}) collective-permute-start(bf16[1024,384]{1,0:T(8,128)(2,1)S(1)} %broadcast_select_fusion.4), channel_id=1, source_target_pairs={{2,0},{3,1},{4,6},{5,7},{10,8},{11,9},{12,14},{13,15},{18,16},{19,... | collective-permute-start | bytes 2359304 | tf_op jit(solution)/shard_map/ppermute | solution.py:62
  57.4 35.2 %collective-permute-start.15 = (bf16[1024,384]{1,0:T(8,128)(2,1)S(1)}, bf16[1024,384]{1,0:T(8,128)(2,1)S(1)}, u32[]{:S(2)}, u32[]{:S(2)}) collective-permute-start(bf16[1024,384]{1,0:T(8,128)(2,1)S(1)} %collective-permute-done.14), channel_id=1, source_target_pairs={{4,6},{5,7},{12,14},{13,15},{20,22},{21,23},{28,30},{29,31}} | collective-permute-start | bytes 2359304 | tf_op jit(solution)/shard_map/ppermute | solution.py:62
  58.8 39.8 %collective-permute-start.10 = (bf16[1024,256]{1,0:T(8,128)(2,1)S(1)}, bf16[1024,256]{1,0:T(8,128)(2,1)S(1)}, u32[]{:S(2)}, u32[]{:S(2)}) collective-permute-start(bf16[1024,256]{1,0:T(8,128)(2,1)S(1)} %pad_maximum_fusion.3), channel_id=1, source_target_pairs={{0,1},{1,0},{2,3},{3,2},{4,5},{5,4},{6,7},{7,6},{8,9},{9,8},{10,11... | collective-permute-start | bytes 1572872 | tf_op jit(solution)/shard_map/ppermute | solution.py:62
  59.7 48.9 %collective-permute-start.19 = (bf16[1024,384]{1,0:T(8,128)(2,1)S(1)}, bf16[1024,384]{1,0:T(8,128)(2,1)S(1)}, u32[]{:S(2)}, u32[]{:S(2)}) collective-permute-start(bf16[1024,384]{1,0:T(8,128)(2,1)S(1)} %broadcast_select_fusion.3), channel_id=1, source_target_pairs={{2,0},{3,1},{4,6},{5,7},{10,8},{11,9},{12,14},{13,15},{18,16},{19,... | collective-permute-start | bytes 2359304 | tf_op jit(solution)/shard_map/ppermute | solution.py:62
  78.4 17.4 %collective-permute-start.20 = (bf16[1024,384]{1,0:T(8,128)(2,1)S(1)}, bf16[1024,384]{1,0:T(8,128)(2,1)S(1)}, u32[]{:S(2)}, u32[]{:S(2)}) collective-permute-start(bf16[1024,384]{1,0:T(8,128)(2,1)S(1)} %collective-permute-done.18), channel_id=1, source_target_pairs={{2,4},{3,5},{10,12},{11,13},{18,20},{19,21},{26,28},{27,29}} | collective-permute-start | bytes 2359304 | tf_op jit(solution)/shard_map/ppermute | solution.py:62
  92.6 41.6 %collective-permute-start.25 = (bf16[1024,128]{1,0:T(8,128)(2,1)S(1)}, bf16[1024,128]{1,0:T(8,128)(2,1)S(1)}, u32[]{:S(2)}, u32[]{:S(2)}) collective-permute-start(bf16[1024,128]{1,0:T(8,128)(2,1)S(1)} %broadcast_select_fusion.9), channel_id=1, source_target_pairs={{2,0},{3,1},{4,6},{5,7},{10,8},{11,9},{12,14},{13,15},{18,16},{19,... | collective-permute-start | bytes 786440 | tf_op jit(solution)/shard_map/ppermute | solution.py:62
  95.9 33.8 %collective-permute-start.16 = (bf16[1024,768]{1,0:T(8,128)(2,1)S(1)}, bf16[1024,768]{1,0:T(8,128)(2,1)S(1)}, u32[]{:S(2)}, u32[]{:S(2)}) collective-permute-start(bf16[1024,768]{1,0:T(8,128)(2,1)S(1)} %pad_maximum_fusion.1), channel_id=1, source_target_pairs={{0,1},{1,0},{2,3},{3,2},{4,5},{5,4},{6,7},{7,6},{8,9},{9,8},{10,11... | collective-permute-start | bytes 4718600 | tf_op jit(solution)/shard_map/ppermute | solution.py:62
  95.9 33.1 %collective-permute-start.21 = (bf16[1024,384]{1,0:T(8,128)(2,1)S(1)}, bf16[1024,384]{1,0:T(8,128)(2,1)S(1)}, u32[]{:S(2)}, u32[]{:S(2)}) collective-permute-start(bf16[1024,384]{1,0:T(8,128)(2,1)S(1)} %collective-permute-done.20), channel_id=1, source_target_pairs={{4,6},{5,7},{12,14},{13,15},{20,22},{21,23},{28,30},{29,31}} | collective-permute-start | bytes 2359304 | tf_op jit(solution)/shard_map/ppermute | solution.py:62
  98.6 10.5 %collective-permute-start.26 = (bf16[1024,128]{1,0:T(8,128)(2,1)S(1)}, bf16[1024,128]{1,0:T(8,128)(2,1)S(1)}, u32[]{:S(2)}, u32[]{:S(2)}) collective-permute-start(bf16[1024,128]{1,0:T(8,128)(2,1)S(1)} %collective-permute-done.24), channel_id=1, source_target_pairs={{2,4},{3,5},{10,12},{11,13},{18,20},{19,21},{26,28},{27,29}} | collective-permute-start | bytes 786440 | tf_op jit(solution)/shard_map/ppermute | solution.py:62
  108.6 21.0 %collective-permute-start.11 = (bf16[128,1024]{1,0:T(8,128)(2,1)S(1)}, bf16[128,1024]{1,0:T(8,128)(2,1)S(1)}, u32[]{:S(2)}, u32[]{:S(2)}) collective-permute-start(bf16[128,1024]{1,0:T(8,128)(2,1)S(1)} %slice.83), channel_id=1, source_target_pairs={{0,16},{1,17},{2,18},{3,19},{4,20},{5,21},{6,22},{7,23},{8,24},{9,... | collective-permute-start | bytes 786440 | tf_op jit(solution)/shard_map/ppermute | solution.py:62
  109.1 25.1 %collective-permute-start.27 = (bf16[1024,128]{1,0:T(8,128)(2,1)S(1)}, bf16[1024,128]{1,0:T(8,128)(2,1)S(1)}, u32[]{:S(2)}, u32[]{:S(2)}) collective-permute-start(bf16[1024,128]{1,0:T(8,128)(2,1)S(1)} %collective-permute-done.26), channel_id=1, source_target_pairs={{4,6},{5,7},{12,14},{13,15},{20,22},{21,23},{28,30},{29,31}} | collective-permute-start | bytes 786440 | tf_op jit(solution)/shard_map/ppermute | solution.py:62
  129.6 23.9 %collective-permute-start.22 = (bf16[1024,768]{1,0:T(8,128)(2,1)S(1)}, bf16[1024,768]{1,0:T(8,128)(2,1)S(1)}, u32[]{:S(2)}, u32[]{:S(2)}) collective-permute-start(bf16[1024,768]{1,0:T(8,128)(2,1)S(1)} %pad_maximum_fusion.2), channel_id=1, source_target_pairs={{0,1},{1,0},{2,3},{3,2},{4,5},{5,4},{6,7},{7,6},{8,9},{9,8},{10,11... | collective-permute-start | bytes 4718600 | tf_op jit(solution)/shard_map/ppermute | solution.py:62
  133.5 20.0 %collective-permute-start.17 = (bf16[384,1024]{1,0:T(8,128)(2,1)S(1)}, bf16[384,1024]{1,0:T(8,128)(2,1)S(1)}, u32[]{:S(2)}, u32[]{:S(2)}) collective-permute-start(bf16[384,1024]{1,0:T(8,128)(2,1)S(1)} %slice.81), channel_id=1, source_target_pairs={{0,16},{1,17},{2,18},{3,19},{4,20},{5,21},{6,22},{7,23},{8,24},{9,... | collective-permute-start | bytes 2359304 | tf_op jit(solution)/shard_map/ppermute | solution.py:62
  153.5 4.5 %collective-permute-start.28 = (bf16[1024,256]{1,0:T(8,128)(2,1)S(1)}, bf16[1024,256]{1,0:T(8,128)(2,1)S(1)}, u32[]{:S(2)}, u32[]{:S(2)}) collective-permute-start(bf16[1024,256]{1,0:T(8,128)(2,1)S(1)} %pad_maximum_fusion.4), channel_id=1, source_target_pairs={{0,1},{1,0},{2,3},{3,2},{4,5},{5,4},{6,7},{7,6},{8,9},{9,8},{10,11... | collective-permute-start | bytes 1572872 | tf_op jit(solution)/shard_map/ppermute | solution.py:62
  157.5 25.7 %collective-permute-start.23 = (bf16[384,1024]{1,0:T(8,128)(2,1)S(1)}, bf16[384,1024]{1,0:T(8,128)(2,1)S(1)}, u32[]{:S(2)}, u32[]{:S(2)}) collective-permute-start(bf16[384,1024]{1,0:T(8,128)(2,1)S(1)} %slice.80), channel_id=1, source_target_pairs={{0,16},{1,17},{2,18},{3,19},{4,20},{5,21},{6,22},{7,23},{8,24},{9,... | collective-permute-start | bytes 2359304 | tf_op jit(solution)/shard_map/ppermute | solution.py:62
  159.6 23.6 %collective-permute-start.29 = (bf16[128,1024]{1,0:T(8,128)(2,1)S(1)}, bf16[128,1024]{1,0:T(8,128)(2,1)S(1)}, u32[]{:S(2)}, u32[]{:S(2)}) collective-permute-start(bf16[128,1024]{1,0:T(8,128)(2,1)S(1)} %slice.82), channel_id=1, source_target_pairs={{0,16},{1,17},{2,18},{3,19},{4,20},{5,21},{6,22},{7,23},{8,24},{9,... | collective-permute-start | bytes 786440 | tf_op jit(solution)/shard_map/ppermute | solution.py:62
  (8 other events, 29.1 us)

commit v2 on v1

--- a/solution.py
+++ b/solution.py
@@ -69,7 +69,7 @@
 def cuts_of(cols):
     unit = cols // 8
     at, out = 0, []
-    for width in (1, 3, 3, 1):
+    for width in (2, 2, 2, 2):
         out.append((at, at + width * unit))
         at += width * unit
     return out
@@ -86,18 +86,13 @@
         return jnp.where(live, block, jnp.zeros_like(block))
 
     n = len(cuts)
-    pieces = [keep(playlist_items[:, lo:hi]) for lo, hi in cuts]
+    w_near = send(playlist_weights, SWAP_X)
+    lead = 3
+    base = [send(keep(playlist_items[:, lo:hi]), ACROSS) for lo, hi in cuts[:lead]]
+    rest = cuts[lead][0]
+    tail = send(after(keep(playlist_items[:, rest:]), w_near), ACROSS)
+    base += [tail[:, lo - rest : hi - rest] for lo, hi in cuts[lead:]]
     own = keep(playlist_items)
-    w_near = send(playlist_weights, SWAP_X)
-    base, up, up2, out, out2 = [], [], [], [], []
-    for j in range(n):
-        base.append(send(after(pieces[j], base[j - 2]) if j >= 2 else after(pieces[j], w_near), ACROSS))
-    near = send(after(own, w_near, *base), SWAP_X)
-    for j in range(n):
-        up.append(send(after(base[j], up[j - 1]) if j >= 2 else base[j], ONE_UP))
-        up2.append(send(after(up[j], up2[j - 1]) if j >= 1 else up[j], ONE_TO_TWO))
-        out.append(send(jnp.where(z == 1, base[j], up[j]), OUTWARD))
-        out2.append(send(up2[j], TWO_TO_THREE))
 
     def scale(block, weight):
         return (weight[:, None].astype(jnp.float32) * block.astype(jnp.float32)).astype(jnp.bfloat16)
@@ -105,7 +100,33 @@
     def dot(lhs, rhs):
         return lax.dot_general(lhs, rhs, (((0,), (0,)), ((), ())), preferred_element_type=jnp.float32)
 
-    here, there = scale(own, playlist_weights), scale(near, w_near)
+    order = [(0, 0), (1, 0)]
+    for j in range(2, n):
+        order += [(j - 2, 1), (j, 0)]
+    order += [(n - 2, 1), (n - 1, 1)]
+    up, out = {}, {}
+    for i, (j, leg) in enumerate(order):
+        value = up[j, 0] if leg else base[j]
+        ties = [up[order[i - 3]]] if i >= 3 else []
+        if i >= 3:
+            ties.append(out[order[i - 3]])
+        if i == 5:
+            ties.append(near[0])
+        up[j, leg] = send(after(value, *ties) if ties else value, ONE_TO_TWO if leg else ONE_UP)
+        if i == 1:
+            near = []
+            for h in range(1):
+                ties = [w_near, up[order[i]]] if h == 0 else [near[h - 1]]
+                near.append(send(after(own[:, h * (cols // 1) : (h + 1) * (cols // 1)], *ties), SWAP_X))
+
+        if leg:
+            out[j, 1] = send(up[j, 1], TWO_TO_THREE)
+        else:
+            out[j, 0] = send(jnp.where(z == 1, base[j], up[j, 0]), OUTWARD)
+    up, up2 = [up[j, 0] for j in range(n)], [up[j, 1] for j in range(n)]
+    out, out2 = [out[j, 0] for j in range(n)], [out[j, 1] for j in range(n)]
+
+    here, there = scale(own, playlist_weights), scale(jnp.concatenate(near, 1), w_near)
     by_mine, by_their = jnp.where(k == x, here, there), jnp.where(k == x, there, here)
     outs, fars = [], []
     for j, (lo, hi) in enumerate(cuts):

time: 189 us -> 169 us (0.89)
  waiting for transfers between devices: 134 us -> 106 us
  other arithmetic: 13.2 us -> 18.4 us
  starting transfers between devices: 26.5 us -> 28.5 us
    ppermute x30, waiting for transfers between devices: 134 us -> 106 us  [send(): return lax.ppermute(value, ('row', 'col'), perm)]
    ppermute x30, starting transfers between devices: 26.5 us -> 28.5 us  [send(): return lax.ppermute(value, ('row', 'col'), perm)]
    select_n x4, other arithmetic: 1.44 us -> 3.38 us  [per_device(): out[j, 0] = send(jnp.where(z == 1, base[j], up[j, 0]), OUTWARD)]
    select_n x3 -> x2, other arithmetic: 3.31 us -> 4.11 us  [keep(): return jnp.where(live, block, jnp.zeros_like(block))]
  transfers between devices with their start and end apart: 30 -> 30, of which waited for: 9 -> 11; matrix products, arithmetic and copies ran while one was open for 11% -> 14% of each run, Pallas kernels for 0% -> 0%
where the time goes in v2:
time: 169 us; the launch traced here: 166 us
  waiting for transfers between devices  106 us (63%)
  starting transfers between devices  28.5 us (17%)
  other arithmetic  18.4 us (11%)
  matrix products  10.2 us (6%)
  local copies, waits for them, and re-layouts  1.87 us (1%)
    ppermute x30, waiting for transfers between devices, send(): return lax.ppermute(value, ('row', 'col'), perm)  106 us
    ppermute x30, starting transfers between devices, send(): return lax.ppermute(value, ('row', 'col'), perm)  28.5 us
    dot_general x8, matrix products, dot(): lax.dot_general(lhs, rhs, (((0,), (0,)), ((), ())), preferred_element_typ...  10.2 us
    select_n x4, other arithmetic, per_device(): jnp.where(y == 1, high, low)  4.52 us
    select_n x2, other arithmetic, keep(): return jnp.where(live, block, jnp.zeros_like(block))  4.11 us
  transfers between devices with their start and end apart: 30, of which 11 were waited for; matrix products, arithmetic and copies ran while one was open for 14% of the time, Pallas kernels for 0%

profile of v2, /device:TPU:30, one launch (start us, length us, event | category | flops | bytes accessed | tf_op | source)
XLA Modules:
  0.0 166.4 jit_solution(2728334262715235463)
XLA Ops:
  0.7 2.7 %slice_select_fusion.1 = (bf16[1024,256]{1,0:T(8,128)(2,1)}, bf16[1024,256]{1,0:T(8,128)(2,1)S(1)}, bf16[1024,256]{1,0:T(8,128)(2,1)S(1)}, bf16[1024,256]{1,0:T(8,128)(2,1)}) fusion(bf16[1024,1024]{1,0:T(8,128)(2,1)} %param.3, pred[]{:T(512)} %bitcast), kind=kLoop, calls=%fused_computation.31 | loop fusion | flops 1048576 | bytes 4194305 | tf_op jit(solution)/shard_map/jit(_where)/select_n | solution.py:86
  3.3 1.6 collective-permute-start
  5.6 1.5 collective-permute-start.1
  7.1 1.4 collective-permute-start.7
  14.1 1.5 collective-permute-start.3
  16.1 23.6 %collective-permute-done.2 = bf16[1024,256]{1,0:T(8,128)(2,1)S(1)} collective-permute-done((bf16[1024,256]{1,0:T(8,128)(2,1)S(1)}, bf16[1024,256]{1,0:T(8,128)(2,1)S(1)}, u32[]{:S(2)}, u32[]{:S(2)}) %collective-permute-start.2) | collective-permute-done | bytes 524320 | tf_op jit(solution)/shard_map/ppermute | solution.py:62
  40.5 1.5 collective-permute-start.17
  42.0 1.5 broadcast_select_fusion
  43.4 1.9 %collective-permute-done.11 = bf16[1024,256]{1,0:T(8,128)(2,1)S(1)} collective-permute-done((bf16[1024,256]{1,0:T(8,128)(2,1)S(1)}, bf16[1024,256]{1,0:T(8,128)(2,1)S(1)}, u32[]{:S(2)}, u32[]{:S(2)}) %collective-permute-start.11) | collective-permute-done | bytes 524320 | tf_op jit(solution)/shard_map/ppermute | solution.py:62
  46.1 1.5 collective-permute-start.12
  53.4 10.6 %collective-permute-done.4 = bf16[1024,256]{1,0:T(8,128)(2,1)} collective-permute-done((bf16[1024,256]{1,0:T(8,128)(2,1)}, bf16[1024,256]{1,0:T(8,128)(2,1)}, u32[]{:S(2)}, u32[]{:S(2)}) %collective-permute-start.4) | collective-permute-done | bytes 524320 | tf_op jit(solution)/shard_map/ppermute | solution.py:62
  64.0 1.8 %broadcast_select_fusion.14 = (bf16[1024,256]{1,0:T(8,128)(2,1)S(1)}, bf16[1024,256]{1,0:T(8,128)(2,1)S(1)}, bf16[1024,256]{1,0:T(8,128)(2,1)S(1)}) fusion(pred[]{:T(512)S(6)} %eq.13, bf16[1024,256]{1,0:T(8,128)(2,1)} %collective-permute-done, bf16[1024,256]{1,0:T(8,128)(2,1)} %collective-permute-done.1, bf16[1024,256]{1,0:T(8,128)(2,1)} %copy-done.3, ...), kind=kLoop, calls=%fused_computation.49 | loop fusion | flops 1572864 | bytes 4194308 | tf_op jit(solution)/shard_map/jit(_where)/select_n | solution.py:135
  66.8 9.9 %collective-permute-done.18 = bf16[1024,256]{1,0:T(8,128)(2,1)S(1)} collective-permute-done((bf16[1024,256]{1,0:T(8,128)(2,1)S(1)}, bf16[1024,256]{1,0:T(8,128)(2,1)S(1)}, u32[]{:S(2)}, u32[]{:S(2)}) %collective-permute-start.18) | collective-permute-done | bytes 524320 | tf_op jit(solution)/shard_map/ppermute | solution.py:62
  77.4 9.6 %collective-permute-done.13 = bf16[1024,256]{1,0:T(8,128)(2,1)S(1)} collective-permute-done((bf16[1024,256]{1,0:T(8,128)(2,1)}, bf16[1024,256]{1,0:T(8,128)(2,1)S(1)}, u32[]{:S(2)}, u32[]{:S(2)}) %collective-permute-start.13) | collective-permute-done | bytes 524320 | tf_op jit(solution)/shard_map/ppermute | solution.py:62
  88.6 2.5 %collective-permute-done.8 = bf16[1024,1024]{1,0:T(8,128)(2,1)} collective-permute-done((bf16[1024,1024]{1,0:T(8,128)(2,1)}, bf16[1024,1024]{1,0:T(8,128)(2,1)}, u32[]{:S(2)}, u32[]{:S(2)}) %collective-permute-start.8) | collective-permute-done | bytes 2097184 | tf_op jit(solution)/shard_map/ppermute | solution.py:62
  91.8 2.5 %broadcast_select_fusion.2 = (bf16[1024,1024]{1,0:T(8,128)(2,1)S(1)}, bf16[1024,1024]{1,0:T(8,128)(2,1)S(1)}) fusion(pred[]{:T(512)S(6)} %eq.17, f32[1024]{0:T(1024)S(1)} %convert_element_type.36, bf16[1024,1024]{1,0:T(8,128)(2,1)} %collective-permute-done.8, f32[1024]{0:T(1024)S(1)} %convert_element_type.39, bf16[1024,1024]{1,0:T(8,128)(2,1)S(1)} %copy-done, ...), kind=kLoop, calls=%fused_computation.5 | loop fusion | flops 9437184 | bytes 8396802 | tf_op jit(solution)/shard_map/jit(_where)/select_n | solution.py:130
  100.9 11.4 %collective-permute-done.20 = bf16[1024,256]{1,0:T(8,128)(2,1)S(1)} collective-permute-done((bf16[1024,256]{1,0:T(8,128)(2,1)S(1)}, bf16[1024,256]{1,0:T(8,128)(2,1)S(1)}, u32[]{:S(2)}, u32[]{:S(2)}) %collective-permute-start.20) | collective-permute-done | bytes 524320 | tf_op jit(solution)/shard_map/ppermute | solution.py:62
  113.8 1.5 collective-permute-start.27
  118.5 5.1 %collective-permute-done.25 = bf16[1024,256]{1,0:T(8,128)(2,1)S(1)} collective-permute-done((bf16[1024,256]{1,0:T(8,128)(2,1)S(1)}, bf16[1024,256]{1,0:T(8,128)(2,1)S(1)}, u32[]{:S(2)}, u32[]{:S(2)}) %collective-permute-start.25) | collective-permute-done | bytes 524320 | tf_op jit(solution)/shard_map/ppermute | solution.py:62
  123.6 11.2 %collective-permute-done.27 = bf16[1024,256]{1,0:T(8,128)(2,1)S(1)} collective-permute-done((bf16[1024,256]{1,0:T(8,128)(2,1)S(1)}, bf16[1024,256]{1,0:T(8,128)(2,1)S(1)}, u32[]{:S(2)}, u32[]{:S(2)}) %collective-permute-start.27) | collective-permute-done | bytes 524320 | tf_op jit(solution)/shard_map/ppermute | solution.py:62
  141.2 1.6 collective-permute-start.29
  143.0 9.8 %collective-permute-done.22 = bf16[256,1024]{1,0:T(8,128)(2,1)S(1)} collective-permute-done((bf16[256,1024]{1,0:T(8,128)(2,1)S(1)}, bf16[256,1024]{1,0:T(8,128)(2,1)S(1)}, u32[]{:S(2)}, u32[]{:S(2)}) %collective-permute-start.22) | collective-permute-done | bytes 524320 | tf_op jit(solution)/shard_map/ppermute | solution.py:62
  153.0 10.7 %collective-permute-done.29 = bf16[256,1024]{1,0:T(8,128)(2,1)S(1)} collective-permute-done((bf16[256,1024]{1,0:T(8,128)(2,1)S(1)}, bf16[256,1024]{1,0:T(8,128)(2,1)S(1)}, u32[]{:S(2)}, u32[]{:S(2)}) %collective-permute-start.29) | collective-permute-done | bytes 524320 | tf_op jit(solution)/shard_map/ppermute | solution.py:62
  163.8 2.6 %pad_maximum_fusion = f32[1024,1024]{1,0:T(8,128)} fusion(f32[256,1024]{1,0:T(8,128)S(1)} %fusion, f32[256,1024]{1,0:T(8,128)S(1)} %fusion.1, f32[256,1024]{1,0:T(8,128)S(1)} %fusion.2, f32[256,1024]{1,0:T(8,128)S(1)} %fusion.3), kind=kLoop, calls=%fused_computation | loop fusion | flops 3145728 | bytes 8388608 | tf_op jit(solution)/shard_map/concatenate | solution.py:143
  (84 shorter events, 35.9 us)
Async XLA Ops:
  8.5 7.6 %collective-permute-start.16 = (bf16[1024,256]{1,0:T(8,128)(2,1)}, bf16[1024,256]{1,0:T(8,128)(2,1)S(1)}, u32[]{:S(2)}, u32[]{:S(2)}) collective-permute-start(bf16[1024,256]{1,0:T(8,128)(2,1)} %get-tuple-element.37), channel_id=1, source_target_pairs={{0,0},{1,8},{2,2},{3,10},{8,1},{9,9},{10,3},{11,11},{16,16},{17,24... | collective-permute-start | bytes 1572872 | tf_op jit(solution)/shard_map/ppermute | solution.py:62
  10.4 29.3 %collective-permute-start.2 = (bf16[1024,256]{1,0:T(8,128)(2,1)S(1)}, bf16[1024,256]{1,0:T(8,128)(2,1)S(1)}, u32[]{:S(2)}, u32[]{:S(2)}) collective-permute-start(bf16[1024,256]{1,0:T(8,128)(2,1)S(1)} %broadcast_select_fusion.6), channel_id=1, source_target_pairs={{2,0},{3,1},{4,6},{5,7},{10,8},{11,9},{12,14},{13,15},{18,16},{19,... | collective-permute-start | bytes 1572872 | tf_op jit(solution)/shard_map/ppermute | solution.py:62
  12.8 32.5 %collective-permute-start.11 = (bf16[1024,256]{1,0:T(8,128)(2,1)S(1)}, bf16[1024,256]{1,0:T(8,128)(2,1)S(1)}, u32[]{:S(2)}, u32[]{:S(2)}) collective-permute-start(bf16[1024,256]{1,0:T(8,128)(2,1)S(1)} %broadcast_select_fusion.5), channel_id=1, source_target_pairs={{2,0},{3,1},{4,6},{5,7},{10,8},{11,9},{12,14},{13,15},{18,16},{19,... | collective-permute-start | bytes 1572872 | tf_op jit(solution)/shard_map/ppermute | solution.py:62
  14.1 33.5 %collective-permute-start.3 = (bf16[1024,256]{1,0:T(8,128)(2,1)}, bf16[1024,256]{1,0:T(8,128)(2,1)}, u32[]{:S(2)}, u32[]{:S(2)}) collective-permute-start(bf16[1024,256]{1,0:T(8,128)(2,1)} %collective-permute-done.1), channel_id=1, source_target_pairs={{2,4},{3,5},{10,12},{11,13},{18,20},{19,21},{26,28},{27,29}} | collective-permute-start | bytes 1572872 | tf_op jit(solution)/shard_map/ppermute | solution.py:62
  15.6 27.8 %collective-permute-start.5 = (s32[1024]{0:T(1024)S(1)}, s32[1024]{0:T(1024)S(1)}, u32[]{:S(2)}, u32[]{:S(2)}) collective-permute-start(s32[1024]{0:T(1024)S(1)} %copy-done.4), channel_id=1, source_target_pairs={{0,8},{1,9},{2,10},{3,11},{4,12},{5,13},{6,14},{7,15},{8,0},{9,1},... | collective-permute-start | bytes 12296 | tf_op jit(solution)/shard_map/ppermute | solution.py:62
  40.5 9.2 %collective-permute-start.17 = (bf16[1024,256]{1,0:T(8,128)(2,1)S(1)}, bf16[1024,256]{1,0:T(8,128)(2,1)}, u32[]{:S(2)}, u32[]{:S(2)}) collective-permute-start(bf16[1024,256]{1,0:T(8,128)(2,1)S(1)} %collective-permute-done.16), channel_id=1, source_target_pairs={{0,2},{1,3},{2,4},{3,5},{8,10},{9,11},{10,12},{11,13},{16,18},{17,... | collective-permute-start | bytes 1572872 | tf_op jit(solution)/shard_map/ppermute | solution.py:62
  43.4 47.7 %collective-permute-start.8 = (bf16[1024,1024]{1,0:T(8,128)(2,1)}, bf16[1024,1024]{1,0:T(8,128)(2,1)}, u32[]{:S(2)}, u32[]{:S(2)}) collective-permute-start(bf16[1024,1024]{1,0:T(8,128)(2,1)} %broadcast_select_fusion), channel_id=1, source_target_pairs={{0,8},{1,9},{2,10},{3,11},{4,12},{5,13},{6,14},{7,15},{8,0},{9,1},... | collective-permute-start | bytes 6291464 | tf_op jit(solution)/shard_map/ppermute | solution.py:62
  47.6 16.4 %collective-permute-start.4 = (bf16[1024,256]{1,0:T(8,128)(2,1)}, bf16[1024,256]{1,0:T(8,128)(2,1)}, u32[]{:S(2)}, u32[]{:S(2)}) collective-permute-start(bf16[1024,256]{1,0:T(8,128)(2,1)} %collective-permute-done.3), channel_id=1, source_target_pairs={{4,6},{5,7},{12,14},{13,15},{20,22},{21,23},{28,30},{29,31}} | collective-permute-start | bytes 1572872 | tf_op jit(solution)/shard_map/ppermute | solution.py:62
  49.0 39.6 %collective-permute-start.23 = (bf16[1024,256]{1,0:T(8,128)(2,1)}, bf16[1024,256]{1,0:T(8,128)(2,1)S(1)}, u32[]{:S(2)}, u32[]{:S(2)}) collective-permute-start(bf16[1024,256]{1,0:T(8,128)(2,1)} %get-tuple-element.19), channel_id=1, source_target_pairs={{0,0},{1,8},{2,2},{3,10},{8,1},{9,9},{10,3},{11,11},{16,16},{17,24... | collective-permute-start | bytes 1572872 | tf_op jit(solution)/shard_map/ppermute | solution.py:62
  50.8 25.9 %collective-permute-start.18 = (bf16[1024,256]{1,0:T(8,128)(2,1)S(1)}, bf16[1024,256]{1,0:T(8,128)(2,1)S(1)}, u32[]{:S(2)}, u32[]{:S(2)}) collective-permute-start(bf16[1024,256]{1,0:T(8,128)(2,1)S(1)} %broadcast_select_fusion.4), channel_id=1, source_target_pairs={{2,0},{3,1},{4,6},{5,7},{10,8},{11,9},{12,14},{13,15},{18,16},{19,... | collective-permute-start | bytes 1572872 | tf_op jit(solution)/shard_map/ppermute | solution.py:62
  52.1 34.9 %collective-permute-start.13 = (bf16[1024,256]{1,0:T(8,128)(2,1)}, bf16[1024,256]{1,0:T(8,128)(2,1)S(1)}, u32[]{:S(2)}, u32[]{:S(2)}) collective-permute-start(bf16[1024,256]{1,0:T(8,128)(2,1)} %collective-permute-done.12), channel_id=1, source_target_pairs={{4,6},{5,7},{12,14},{13,15},{20,22},{21,23},{28,30},{29,31}} | collective-permute-start | bytes 1572872 | tf_op jit(solution)/shard_map/ppermute | solution.py:62
  66.0 28.4 %collective-permute-start.9 = (bf16[1024,512]{1,0:T(8,128)(2,1)S(1)}, bf16[1024,512]{1,0:T(8,128)(2,1)S(1)}, u32[]{:S(2)}, u32[]{:S(2)}) collective-permute-start(bf16[1024,512]{1,0:T(8,128)(2,1)S(1)} %pad_maximum_fusion.1), channel_id=1, source_target_pairs={{0,1},{1,0},{2,3},{3,2},{4,5},{5,4},{6,7},{7,6},{8,9},{9,8},{10,11... | collective-permute-start | bytes 3145736 | tf_op jit(solution)/shard_map/ppermute | solution.py:62
  76.7 18.9 %collective-permute-start.19 = (bf16[1024,256]{1,0:T(8,128)(2,1)}, bf16[1024,256]{1,0:T(8,128)(2,1)S(1)}, u32[]{:S(2)}, u32[]{:S(2)}) collective-permute-start(bf16[1024,256]{1,0:T(8,128)(2,1)} %collective-permute-done.17), channel_id=1, source_target_pairs={{2,4},{3,5},{10,12},{11,13},{18,20},{19,21},{26,28},{27,29}} | collective-permute-start | bytes 1572872 | tf_op jit(solution)/shard_map/ppermute | solution.py:62
  88.5 26.8 %collective-permute-start.14 = (bf16[1024,512]{1,0:T(8,128)(2,1)S(1)}, bf16[1024,512]{1,0:T(8,128)(2,1)S(1)}, u32[]{:S(2)}, u32[]{:S(2)}) collective-permute-start(bf16[1024,512]{1,0:T(8,128)(2,1)S(1)} %pad_maximum_fusion.2), channel_id=1, source_target_pairs={{0,1},{1,0},{2,3},{3,2},{4,5},{5,4},{6,7},{7,6},{8,9},{9,8},{10,11... | collective-permute-start | bytes 3145736 | tf_op jit(solution)/shard_map/ppermute | solution.py:62
  91.1 7.8 %collective-permute-start.24 = (bf16[1024,256]{1,0:T(8,128)(2,1)S(1)}, bf16[1024,256]{1,0:T(8,128)(2,1)S(1)}, u32[]{:S(2)}, u32[]{:S(2)}) collective-permute-start(bf16[1024,256]{1,0:T(8,128)(2,1)S(1)} %collective-permute-done.23), channel_id=1, source_target_pairs={{0,2},{1,3},{2,4},{3,5},{8,10},{9,11},{10,12},{11,13},{16,18},{17,... | collective-permute-start | bytes 1572872 | tf_op jit(solution)/shard_map/ppermute | solution.py:62
  95.6 16.7 %collective-permute-start.20 = (bf16[1024,256]{1,0:T(8,128)(2,1)S(1)}, bf16[1024,256]{1,0:T(8,128)(2,1)S(1)}, u32[]{:S(2)}, u32[]{:S(2)}) collective-permute-start(bf16[1024,256]{1,0:T(8,128)(2,1)S(1)} %collective-permute-done.19), channel_id=1, source_target_pairs={{4,6},{5,7},{12,14},{13,15},{20,22},{21,23},{28,30},{29,31}} | collective-permute-start | bytes 1572872 | tf_op jit(solution)/shard_map/ppermute | solution.py:62
  98.3 15.4 %collective-permute-start.10 = (bf16[256,1024]{1,0:T(8,128)(2,1)S(1)}, bf16[256,1024]{1,0:T(8,128)(2,1)S(1)}, u32[]{:S(2)}, u32[]{:S(2)}) collective-permute-start(bf16[256,1024]{1,0:T(8,128)(2,1)S(1)} %slice.83), channel_id=1, source_target_pairs={{0,16},{1,17},{2,18},{3,19},{4,20},{5,21},{6,22},{7,23},{8,24},{9,... | collective-permute-start | bytes 1572872 | tf_op jit(solution)/shard_map/ppermute | solution.py:62
  98.9 24.6 %collective-permute-start.25 = (bf16[1024,256]{1,0:T(8,128)(2,1)S(1)}, bf16[1024,256]{1,0:T(8,128)(2,1)S(1)}, u32[]{:S(2)}, u32[]{:S(2)}) collective-permute-start(bf16[1024,256]{1,0:T(8,128)(2,1)S(1)} %broadcast_select_fusion.3), channel_id=1, source_target_pairs={{2,0},{3,1},{4,6},{5,7},{10,8},{11,9},{12,14},{13,15},{18,16},{19,... | collective-permute-start | bytes 1572872 | tf_op jit(solution)/shard_map/ppermute | solution.py:62
  100.2 13.6 %collective-permute-start.26 = (bf16[1024,256]{1,0:T(8,128)(2,1)S(1)}, bf16[1024,256]{1,0:T(8,128)(2,1)S(1)}, u32[]{:S(2)}, u32[]{:S(2)}) collective-permute-start(bf16[1024,256]{1,0:T(8,128)(2,1)S(1)} %collective-permute-done.24), channel_id=1, source_target_pairs={{2,4},{3,5},{10,12},{11,13},{18,20},{19,21},{26,28},{27,29}} | collective-permute-start | bytes 1572872 | tf_op jit(solution)/shard_map/ppermute | solution.py:62
  113.7 21.7 %collective-permute-start.21 = (bf16[1024,512]{1,0:T(8,128)(2,1)S(1)}, bf16[1024,512]{1,0:T(8,128)(2,1)S(1)}, u32[]{:S(2)}, u32[]{:S(2)}) collective-permute-start(bf16[1024,512]{1,0:T(8,128)(2,1)S(1)} %pad_maximum_fusion.3), channel_id=1, source_target_pairs={{0,1},{1,0},{2,3},{3,2},{4,5},{5,4},{6,7},{7,6},{8,9},{9,8},{10,11... | collective-permute-start | bytes 3145736 | tf_op jit(solution)/shard_map/ppermute | solution.py:62
  113.8 20.9 %collective-permute-start.27 = (bf16[1024,256]{1,0:T(8,128)(2,1)S(1)}, bf16[1024,256]{1,0:T(8,128)(2,1)S(1)}, u32[]{:S(2)}, u32[]{:S(2)}) collective-permute-start(bf16[1024,256]{1,0:T(8,128)(2,1)S(1)} %collective-permute-done.26), channel_id=1, source_target_pairs={{4,6},{5,7},{12,14},{13,15},{20,22},{21,23},{28,30},{29,31}} | collective-permute-start | bytes 1572872 | tf_op jit(solution)/shard_map/ppermute | solution.py:62
  117.9 17.1 %collective-permute-start.15 = (bf16[256,1024]{1,0:T(8,128)(2,1)S(1)}, bf16[256,1024]{1,0:T(8,128)(2,1)S(1)}, u32[]{:S(2)}, u32[]{:S(2)}) collective-permute-start(bf16[256,1024]{1,0:T(8,128)(2,1)S(1)} %slice.82), channel_id=1, source_target_pairs={{0,16},{1,17},{2,18},{3,19},{4,20},{5,21},{6,22},{7,23},{8,24},{9,... | collective-permute-start | bytes 1572872 | tf_op jit(solution)/shard_map/ppermute | solution.py:62
  138.0 14.8 %collective-permute-start.22 = (bf16[256,1024]{1,0:T(8,128)(2,1)S(1)}, bf16[256,1024]{1,0:T(8,128)(2,1)S(1)}, u32[]{:S(2)}, u32[]{:S(2)}) collective-permute-start(bf16[256,1024]{1,0:T(8,128)(2,1)S(1)} %slice.81), channel_id=1, source_target_pairs={{0,16},{1,17},{2,18},{3,19},{4,20},{5,21},{6,22},{7,23},{8,24},{9,... | collective-permute-start | bytes 1572872 | tf_op jit(solution)/shard_map/ppermute | solution.py:62
  141.2 22.4 %collective-permute-start.29 = (bf16[256,1024]{1,0:T(8,128)(2,1)S(1)}, bf16[256,1024]{1,0:T(8,128)(2,1)S(1)}, u32[]{:S(2)}, u32[]{:S(2)}) collective-permute-start(bf16[256,1024]{1,0:T(8,128)(2,1)S(1)} %slice.80), channel_id=1, source_target_pairs={{0,16},{1,17},{2,18},{3,19},{4,20},{5,21},{6,22},{7,23},{8,24},{9,... | collective-permute-start | bytes 1572872 | tf_op jit(solution)/shard_map/ppermute | solution.py:62
  (11 other events, 95.8 us)

commit v3 on v1

--- a/solution.py
+++ b/solution.py
@@ -69,7 +69,7 @@
 def cuts_of(cols):
     unit = cols // 8
     at, out = 0, []
-    for width in (1, 3, 3, 1):
+    for width in (2, 2, 2, 2):
         out.append((at, at + width * unit))
         at += width * unit
     return out
@@ -86,18 +86,16 @@
         return jnp.where(live, block, jnp.zeros_like(block))
 
     n = len(cuts)
-    pieces = [keep(playlist_items[:, lo:hi]) for lo, hi in cuts]
+    w_near = send(playlist_weights, SWAP_X)
+    base = []
+    for i, (lo, hi) in enumerate(cuts[:3]):
+        block = keep(playlist_items[:, lo:hi])
+        base.append(send(after(block, w_near) if i == 1 else block, ACROSS))
+    rest = cuts[3][0]
+    tail = send(keep(playlist_items[:, rest:]), ACROSS)
+    base += [tail[:, lo - rest : hi - rest] for lo, hi in cuts[3:]]
     own = keep(playlist_items)
-    w_near = send(playlist_weights, SWAP_X)
-    base, up, up2, out, out2 = [], [], [], [], []
-    for j in range(n):
-        base.append(send(after(pieces[j], base[j - 2]) if j >= 2 else after(pieces[j], w_near), ACROSS))
-    near = send(after(own, w_near, *base), SWAP_X)
-    for j in range(n):
-        up.append(send(after(base[j], up[j - 1]) if j >= 2 else base[j], ONE_UP))
-        up2.append(send(after(up[j], up2[j - 1]) if j >= 1 else up[j], ONE_TO_TWO))
-        out.append(send(jnp.where(z == 1, base[j], up[j]), OUTWARD))
-        out2.append(send(up2[j], TWO_TO_THREE))
+    near = send(after(own, w_near, tail), SWAP_X)
 
     def scale(block, weight):
         return (weight[:, None].astype(jnp.float32) * block.astype(jnp.float32)).astype(jnp.bfloat16)
@@ -105,21 +103,43 @@
     def dot(lhs, rhs):
         return lax.dot_general(lhs, rhs, (((0,), (0,)), ((), ())), preferred_element_type=jnp.float32)
 
+    up, out, kept, given, fars = {}, {}, [], [], []
+
+    def finish(j, *ties):
+        lo, hi = cuts[j]
+        high = jnp.where(z == 1, base[j], jnp.where(z == 2, up[j, 0], out[j, 0]))
+        low = jnp.where(z == 0, base[j], jnp.where(z == 1, up[j, 0], up[j, 1] + out[j, 1]))
+        mine = jnp.concatenate([jnp.where(y == 1, high, low), jnp.where(y == 1, low, high)], 1)
+        mine = after(mine, *ties) if ties else mine
+        part = dot(mine, by_mine) + dot(send(mine, CORES), by_their)
+        kept.append(part[: hi - lo])
+        given.append(part[hi - lo :].astype(jnp.bfloat16))
+        fars.append(send(given[j], SWAP_Y))
+
+    up[0, 0] = send(base[0], ONE_UP)
+    out[0, 0] = send(jnp.where(z == 1, base[0], up[0, 0]), OUTWARD)
+    up[1, 0] = send(base[1], ONE_UP)
+    out[1, 0] = send(jnp.where(z == 1, base[1], up[1, 0]), OUTWARD)
+    up[0, 1] = send(up[0, 0], ONE_TO_TWO)
+    out[0, 1] = send(up[0, 1], TWO_TO_THREE)
+    up[2, 0] = send(after(base[2], up[0, 0], out[0, 0]), ONE_UP)
+    out[2, 0] = send(jnp.where(z == 1, base[2], up[2, 0]), OUTWARD)
+    up[1, 1] = send(after(up[1, 0], up[1, 0], out[1, 0]), ONE_TO_TWO)
+    out[1, 1] = send(up[1, 1], TWO_TO_THREE)
+    up[3, 0] = send(after(base[3], up[0, 1], out[0, 1]), ONE_UP)
+    out[3, 0] = send(jnp.where(z == 1, base[3], up[3, 0]), OUTWARD)
+    up[2, 1] = send(after(up[2, 0], up[2, 0], out[2, 0]), ONE_TO_TWO)
+    out[2, 1] = send(up[2, 1], TWO_TO_THREE)
+    up[3, 1] = send(after(up[3, 0], up[1, 1], out[1, 1]), ONE_TO_TWO)
+    out[3, 1] = send(up[3, 1], TWO_TO_THREE)
     here, there = scale(own, playlist_weights), scale(near, w_near)
     by_mine, by_their = jnp.where(k == x, here, there), jnp.where(k == x, there, here)
-    outs, fars = [], []
-    for j, (lo, hi) in enumerate(cuts):
-        high = jnp.where(z == 1, base[j], jnp.where(z == 2, up[j], out[j]))
-        low = jnp.where(z == 0, base[j], jnp.where(z == 1, up[j], up2[j] + out2[j]))
-        mine = jnp.concatenate([jnp.where(y == 1, high, low), jnp.where(y == 1, low, high)], 1)
-        if j >= 2:
-            mine = after(mine, fars[j - 2])
-        their = send(mine, CORES)
-        part = dot(mine, by_mine) + dot(their, by_their)
-        far = send(part[hi - lo :].astype(jnp.bfloat16), SWAP_Y)
-        fars.append(far)
-        outs.append((part[: hi - lo] + far.astype(jnp.float32)) / jnp.float32(4 * rows))
-    return jnp.concatenate(outs, 0)
+    finish(0)
+    finish(1)
+    finish(2, fars[0], given[1])
+    finish(3, fars[1], given[2])
+    sums = [a + b.astype(jnp.float32) for a, b in zip(kept, fars)]
+    return jnp.concatenate(sums, 0) / jnp.float32(4 * rows)
 
 
 def solution(mesh):

time: 189 us -> 163 us (0.86)
  waiting for transfers between devices: 134 us -> 104 us
  other arithmetic: 13.2 us -> 18.7 us
    ppermute x30, waiting for transfers between devices: 134 us -> 104 us  [send(): return lax.ppermute(value, ('row', 'col'), perm)]
    select_n x12, other arithmetic: 4.9 us -> 8.06 us  [the longest x4 4.56 us: finish(): jnp.where(y == 1, high, low)]
    concatenate x5 -> x4, other arithmetic: 2.97 us -> 0.31 us  [finish(): jnp.concatenate([jnp.where(y == 1, high, low), jnp.where(y == 1, low, hig...]
    div x4 -> x1, other arithmetic: 0.6 us -> 2.86 us  [per_device(): return jnp.concatenate(sums, 0) / jnp.float32(4 * rows)]
    select_n x3 -> x2, other arithmetic: 3.31 us -> 4.33 us  [keep(): return jnp.where(live, block, jnp.zeros_like(block))]
  transfers between devices with their start and end apart: 30 -> 30, of which waited for: 9 -> 12; matrix products, arithmetic and copies ran while one was open for 11% -> 14% of each run, Pallas kernels for 0% -> 0%
where the time goes in v3:
time: 163 us; the launch traced here: 162 us
  waiting for transfers between devices  104 us (64%)
  starting transfers between devices  26.3 us (16%)
  other arithmetic  18.7 us (11%)
  matrix products  10.1 us (6%)
    ppermute x30, waiting for transfers between devices, send(): return lax.ppermute(value, ('row', 'col'), perm)  104 us
    ppermute x30, starting transfers between devices, send(): return lax.ppermute(value, ('row', 'col'), perm)  26.3 us
    dot_general x8, matrix products, dot(): lax.dot_general(lhs, rhs, (((0,), (0,)), ((), ())), preferred_element_typ...  10.1 us
    select_n x4, other arithmetic, finish(): jnp.where(y == 1, high, low)  4.56 us
    select_n x2, other arithmetic, keep(): return jnp.where(live, block, jnp.zeros_like(block))  4.33 us
  transfers between devices with their start and end apart: 30, of which 12 were waited for; matrix products, arithmetic and copies ran while one was open for 14% of the time, Pallas kernels for 0%

profile of v3, /device:TPU:30, one launch (start us, length us, event | category | flops | bytes accessed | tf_op | source)
XLA Modules:
  0.0 161.7 jit_solution(1370809862139151240)
XLA Ops:
  0.7 2.9 %slice_select_fusion = (bf16[1024,256]{1,0:T(8,128)(2,1)}, bf16[1024,256]{1,0:T(8,128)(2,1)}, bf16[1024,256]{1,0:T(8,128)(2,1)S(1)}, bf16[1024,256]{1,0:T(8,128)(2,1)}) fusion(bf16[1024,1024]{1,0:T(8,128)(2,1)} %param.3, pred[]{:T(512)} %bitcast), kind=kLoop, calls=%fused_computation.26 | loop fusion | flops 1048576 | bytes 4194305 | tf_op jit(solution)/shard_map/jit(_where)/select_n | solution.py:86
  3.5 1.5 collective-permute-start
  5.6 3.1 %collective-permute-done.5 = s32[1024]{0:T(1024)S(1)} collective-permute-done((s32[1024]{0:T(1024)S(1)}, s32[1024]{0:T(1024)S(1)}, u32[]{:S(2)}, u32[]{:S(2)}) %collective-permute-start.5) | collective-permute-done | bytes 4128 | tf_op jit(solution)/shard_map/ppermute | solution.py:62
  8.6 1.5 collective-permute-start.10
  10.1 1.5 collective-permute-start.1
  16.1 1.5 broadcast_select_fusion
  18.1 1.4 collective-permute-start.3
  21.9 15.1 %collective-permute-done.2 = bf16[1024,256]{1,0:T(8,128)(2,1)S(1)} collective-permute-done((bf16[1024,256]{1,0:T(8,128)(2,1)S(1)}, bf16[1024,256]{1,0:T(8,128)(2,1)S(1)}, u32[]{:S(2)}, u32[]{:S(2)}) %collective-permute-start.2) | collective-permute-done | bytes 524320 | tf_op jit(solution)/shard_map/ppermute | solution.py:62
  37.8 1.5 collective-permute-start.18
  40.6 11.9 %collective-permute-done.12 = bf16[1024,256]{1,0:T(8,128)(2,1)} collective-permute-done((bf16[1024,256]{1,0:T(8,128)(2,1)}, bf16[1024,256]{1,0:T(8,128)(2,1)}, u32[]{:S(2)}, u32[]{:S(2)}) %collective-permute-start.12) | collective-permute-done | bytes 524320 | tf_op jit(solution)/shard_map/ppermute | solution.py:62
  55.6 12.1 %collective-permute-done.4 = bf16[1024,256]{1,0:T(8,128)(2,1)} collective-permute-done((bf16[1024,256]{1,0:T(8,128)(2,1)}, bf16[1024,256]{1,0:T(8,128)(2,1)}, u32[]{:S(2)}, u32[]{:S(2)}) %collective-permute-start.4) | collective-permute-done | bytes 524320 | tf_op jit(solution)/shard_map/ppermute | solution.py:62
  68.4 1.8 %broadcast_select_fusion.14 = (bf16[1024,256]{1,0:T(8,128)(2,1)S(1)}, bf16[1024,256]{1,0:T(8,128)(2,1)S(1)}, bf16[1024,256]{1,0:T(8,128)(2,1)S(1)}) fusion(pred[]{:T(512)S(6)} %eq.13, bf16[1024,256]{1,0:T(8,128)(2,1)} %collective-permute-done, bf16[1024,256]{1,0:T(8,128)(2,1)} %collective-permute-done.1, bf16[1024,256]{1,0:T(8,128)(2,1)} %copy-done.3, ...), kind=kLoop, calls=%fused_computation.45 | loop fusion | flops 1572864 | bytes 4194308 | tf_op jit(solution)/shard_map/jit(_where)/select_n | solution.py:112
  71.8 9.0 %collective-permute-done.19 = bf16[1024,256]{1,0:T(8,128)(2,1)S(1)} collective-permute-done((bf16[1024,256]{1,0:T(8,128)(2,1)S(1)}, bf16[1024,256]{1,0:T(8,128)(2,1)S(1)}, u32[]{:S(2)}, u32[]{:S(2)}) %collective-permute-start.19) | collective-permute-done | bytes 524320 | tf_op jit(solution)/shard_map/ppermute | solution.py:62
  81.6 1.4 collective-permute-start.25
  83.1 2.5 %broadcast_select_fusion.2 = (bf16[1024,1024]{1,0:T(8,128)(2,1)S(1)}, bf16[1024,1024]{1,0:T(8,128)(2,1)S(1)}) fusion(pred[]{:T(512)S(6)} %eq.17, f32[1024]{0:T(1024)S(1)} %convert_element_type.36, bf16[1024,1024]{1,0:T(8,128)(2,1)} %collective-permute-done.7, f32[1024]{0:T(1024)S(1)} %convert_element_type.39, bf16[1024,1024]{1,0:T(8,128)(2,1)S(1)} %copy-done, ...), kind=kLoop, calls=%fused_computation.5 | loop fusion | flops 9437184 | bytes 8396802 | tf_op jit(solution)/shard_map/jit(_where)/select_n | solution.py:136
  85.6 6.4 %collective-permute-done.14 = bf16[1024,256]{1,0:T(8,128)(2,1)S(1)} collective-permute-done((bf16[1024,256]{1,0:T(8,128)(2,1)S(1)}, bf16[1024,256]{1,0:T(8,128)(2,1)S(1)}, u32[]{:S(2)}, u32[]{:S(2)}) %collective-permute-start.14) | collective-permute-done | bytes 524320 | tf_op jit(solution)/shard_map/ppermute | solution.py:62
  98.8 1.5 collective-permute-start.27
  100.3 14.2 %collective-permute-done.21 = bf16[1024,256]{1,0:T(8,128)(2,1)S(1)} collective-permute-done((bf16[1024,256]{1,0:T(8,128)(2,1)S(1)}, bf16[1024,256]{1,0:T(8,128)(2,1)S(1)}, u32[]{:S(2)}, u32[]{:S(2)}) %collective-permute-start.21) | collective-permute-done | bytes 524320 | tf_op jit(solution)/shard_map/ppermute | solution.py:62
  119.1 5.6 %collective-permute-done.27 = bf16[1024,256]{1,0:T(8,128)(2,1)S(1)} collective-permute-done((bf16[1024,256]{1,0:T(8,128)(2,1)S(1)}, bf16[1024,256]{1,0:T(8,128)(2,1)S(1)}, u32[]{:S(2)}, u32[]{:S(2)}) %collective-permute-start.27) | collective-permute-done | bytes 524320 | tf_op jit(solution)/shard_map/ppermute | solution.py:62
  127.7 5.2 %collective-permute-done.16 = bf16[256,1024]{1,0:T(8,128)(2,1)S(1)} collective-permute-done((bf16[256,1024]{1,0:T(8,128)(2,1)S(1)}, bf16[256,1024]{1,0:T(8,128)(2,1)S(1)}, u32[]{:S(2)}, u32[]{:S(2)}) %collective-permute-start.16) | collective-permute-done | bytes 524320 | tf_op jit(solution)/shard_map/ppermute | solution.py:62
  133.6 1.9 %collective-permute-done.28 = bf16[1024,512]{1,0:T(8,128)(2,1)S(1)} collective-permute-done((bf16[1024,512]{1,0:T(8,128)(2,1)S(1)}, bf16[1024,512]{1,0:T(8,128)(2,1)S(1)}, u32[]{:S(2)}, u32[]{:S(2)}) %collective-permute-start.28) | collective-permute-done | bytes 1048608 | tf_op jit(solution)/shard_map/ppermute | solution.py:62
  138.9 9.0 %collective-permute-done.23 = bf16[256,1024]{1,0:T(8,128)(2,1)S(1)} collective-permute-done((bf16[256,1024]{1,0:T(8,128)(2,1)S(1)}, bf16[256,1024]{1,0:T(8,128)(2,1)S(1)}, u32[]{:S(2)}, u32[]{:S(2)}) %collective-permute-start.23) | collective-permute-done | bytes 524320 | tf_op jit(solution)/shard_map/ppermute | solution.py:62
  148.0 10.7 %collective-permute-done.29 = bf16[256,1024]{1,0:T(8,128)(2,1)S(1)} collective-permute-done((bf16[256,1024]{1,0:T(8,128)(2,1)S(1)}, bf16[256,1024]{1,0:T(8,128)(2,1)S(1)}, u32[]{:S(2)}, u32[]{:S(2)}) %collective-permute-start.29) | collective-permute-done | bytes 524320 | tf_op jit(solution)/shard_map/ppermute | solution.py:62
  158.9 2.9 %maximum_multiply_fusion = f32[1024,1024]{1,0:T(8,128)} fusion(f32[256,1024]{1,0:T(8,128)S(1)} %slice_add_fusion, f32[256,1024]{1,0:T(8,128)S(1)} %slice_add_fusion.1, f32[256,1024]{1,0:T(8,128)S(1)} %slice_add_fusion.2, f32[256,1024]{1,0:T(8,128)S(1)} %slice_add_fusion.3), kind=kLoop, calls=%fused_computation | loop fusion | flops 4194304 | bytes 8388608 | tf_op jit(solution)/shard_map/div | solution.py:142
  (84 shorter events, 34.6 us)
Async XLA Ops:
  11.6 10.3 %collective-permute-start.17 = (bf16[1024,256]{1,0:T(8,128)(2,1)}, bf16[1024,256]{1,0:T(8,128)(2,1)S(1)}, u32[]{:S(2)}, u32[]{:S(2)}) collective-permute-start(bf16[1024,256]{1,0:T(8,128)(2,1)} %get-tuple-element.37), channel_id=1, source_target_pairs={{0,0},{1,8},{2,2},{3,10},{8,1},{9,9},{10,3},{11,11},{16,16},{17,24... | collective-permute-start | bytes 1572872 | tf_op jit(solution)/shard_map/ppermute | solution.py:62
  13.0 6.6 %collective-permute-start.11 = (bf16[1024,256]{1,0:T(8,128)(2,1)}, bf16[1024,256]{1,0:T(8,128)(2,1)S(1)}, u32[]{:S(2)}, u32[]{:S(2)}) collective-permute-start(bf16[1024,256]{1,0:T(8,128)(2,1)} %collective-permute-done.10), channel_id=1, source_target_pairs={{0,2},{1,3},{2,4},{3,5},{8,10},{9,11},{10,12},{11,13},{16,18},{17,... | collective-permute-start | bytes 1572872 | tf_op jit(solution)/shard_map/ppermute | solution.py:62
  14.8 22.2 %collective-permute-start.2 = (bf16[1024,256]{1,0:T(8,128)(2,1)S(1)}, bf16[1024,256]{1,0:T(8,128)(2,1)S(1)}, u32[]{:S(2)}, u32[]{:S(2)}) collective-permute-start(bf16[1024,256]{1,0:T(8,128)(2,1)S(1)} %broadcast_select_fusion.6), channel_id=1, source_target_pairs={{2,0},{3,1},{4,6},{5,7},{10,8},{11,9},{12,14},{13,15},{18,16},{19,... | collective-permute-start | bytes 1572872 | tf_op jit(solution)/shard_map/ppermute | solution.py:62
  17.6 65.5 %collective-permute-start.7 = (bf16[1024,1024]{1,0:T(8,128)(2,1)}, bf16[1024,1024]{1,0:T(8,128)(2,1)}, u32[]{:S(2)}, u32[]{:S(2)}) collective-permute-start(bf16[1024,1024]{1,0:T(8,128)(2,1)} %broadcast_select_fusion), channel_id=1, source_target_pairs={{0,8},{1,9},{2,10},{3,11},{4,12},{5,13},{6,14},{7,15},{8,0},{9,1},... | collective-permute-start | bytes 6291464 | tf_op jit(solution)/shard_map/ppermute | solution.py:62
  18.1 21.1 %collective-permute-start.3 = (bf16[1024,256]{1,0:T(8,128)(2,1)}, bf16[1024,256]{1,0:T(8,128)(2,1)}, u32[]{:S(2)}, u32[]{:S(2)}) collective-permute-start(bf16[1024,256]{1,0:T(8,128)(2,1)} %collective-permute-done.1), channel_id=1, source_target_pairs={{2,4},{3,5},{10,12},{11,13},{18,20},{19,21},{26,28},{27,29}} | collective-permute-start | bytes 1572872 | tf_op jit(solution)/shard_map/ppermute | solution.py:62
  20.5 32.0 %collective-permute-start.12 = (bf16[1024,256]{1,0:T(8,128)(2,1)}, bf16[1024,256]{1,0:T(8,128)(2,1)}, u32[]{:S(2)}, u32[]{:S(2)}) collective-permute-start(bf16[1024,256]{1,0:T(8,128)(2,1)} %broadcast_select_fusion.5), channel_id=1, source_target_pairs={{2,0},{3,1},{4,6},{5,7},{10,8},{11,9},{12,14},{13,15},{18,16},{19,... | collective-permute-start | bytes 1572872 | tf_op jit(solution)/shard_map/ppermute | solution.py:62
  37.8 15.4 %collective-permute-start.18 = (bf16[1024,256]{1,0:T(8,128)(2,1)S(1)}, bf16[1024,256]{1,0:T(8,128)(2,1)}, u32[]{:S(2)}, u32[]{:S(2)}) collective-permute-start(bf16[1024,256]{1,0:T(8,128)(2,1)S(1)} %collective-permute-done.17), channel_id=1, source_target_pairs={{0,2},{1,3},{2,4},{3,5},{8,10},{9,11},{10,12},{11,13},{16,18},{17,... | collective-permute-start | bytes 1572872 | tf_op jit(solution)/shard_map/ppermute | solution.py:62
  39.3 28.5 %collective-permute-start.4 = (bf16[1024,256]{1,0:T(8,128)(2,1)}, bf16[1024,256]{1,0:T(8,128)(2,1)}, u32[]{:S(2)}, u32[]{:S(2)}) collective-permute-start(bf16[1024,256]{1,0:T(8,128)(2,1)} %collective-permute-done.3), channel_id=1, source_target_pairs={{4,6},{5,7},{12,14},{13,15},{20,22},{21,23},{28,30},{29,31}} | collective-permute-start | bytes 1572872 | tf_op jit(solution)/shard_map/ppermute | solution.py:62
  52.5 18.0 %collective-permute-start.13 = (bf16[1024,256]{1,0:T(8,128)(2,1)}, bf16[1024,256]{1,0:T(8,128)(2,1)S(1)}, u32[]{:S(2)}, u32[]{:S(2)}) collective-permute-start(bf16[1024,256]{1,0:T(8,128)(2,1)} %copy-done.1), channel_id=1, source_target_pairs={{2,4},{3,5},{10,12},{11,13},{18,20},{19,21},{26,28},{27,29}} | collective-permute-start | bytes 1572872 | tf_op jit(solution)/shard_map/ppermute | solution.py:62
  54.3 26.5 %collective-permute-start.19 = (bf16[1024,256]{1,0:T(8,128)(2,1)S(1)}, bf16[1024,256]{1,0:T(8,128)(2,1)S(1)}, u32[]{:S(2)}, u32[]{:S(2)}) collective-permute-start(bf16[1024,256]{1,0:T(8,128)(2,1)S(1)} %broadcast_select_fusion.4), channel_id=1, source_target_pairs={{2,0},{3,1},{4,6},{5,7},{10,8},{11,9},{12,14},{13,15},{18,16},{19,... | collective-permute-start | bytes 1572872 | tf_op jit(solution)/shard_map/ppermute | solution.py:62
  67.8 13.8 %collective-permute-start.24 = (bf16[1024,256]{1,0:T(8,128)(2,1)S(1)}, bf16[1024,256]{1,0:T(8,128)(2,1)S(1)}, u32[]{:S(2)}, u32[]{:S(2)}) collective-permute-start(bf16[1024,256]{1,0:T(8,128)(2,1)S(1)} %collective-permute-done.6), channel_id=1, source_target_pairs={{0,2},{1,3},{2,4},{3,5},{8,10},{9,11},{10,12},{11,13},{16,18},{17,... | collective-permute-start | bytes 1572872 | tf_op jit(solution)/shard_map/ppermute | solution.py:62
  70.4 25.2 %collective-permute-start.8 = (bf16[1024,512]{1,0:T(8,128)(2,1)S(1)}, bf16[1024,512]{1,0:T(8,128)(2,1)S(1)}, u32[]{:S(2)}, u32[]{:S(2)}) collective-permute-start(bf16[1024,512]{1,0:T(8,128)(2,1)S(1)} %pad_maximum_fusion), channel_id=1, source_target_pairs={{0,1},{1,0},{2,3},{3,2},{4,5},{5,4},{6,7},{7,6},{8,9},{9,8},{10,11... | collective-permute-start | bytes 3145736 | tf_op jit(solution)/shard_map/ppermute | solution.py:62
  70.5 21.4 %collective-permute-start.14 = (bf16[1024,256]{1,0:T(8,128)(2,1)S(1)}, bf16[1024,256]{1,0:T(8,128)(2,1)S(1)}, u32[]{:S(2)}, u32[]{:S(2)}) collective-permute-start(bf16[1024,256]{1,0:T(8,128)(2,1)S(1)} %collective-permute-done.13), channel_id=1, source_target_pairs={{4,6},{5,7},{12,14},{13,15},{20,22},{21,23},{28,30},{29,31}} | collective-permute-start | bytes 1572872 | tf_op jit(solution)/shard_map/ppermute | solution.py:62
  80.8 13.4 %collective-permute-start.20 = (bf16[1024,256]{1,0:T(8,128)(2,1)}, bf16[1024,256]{1,0:T(8,128)(2,1)S(1)}, u32[]{:S(2)}, u32[]{:S(2)}) collective-permute-start(bf16[1024,256]{1,0:T(8,128)(2,1)} %collective-permute-done.18), channel_id=1, source_target_pairs={{2,4},{3,5},{10,12},{11,13},{18,20},{19,21},{26,28},{27,29}} | collective-permute-start | bytes 1572872 | tf_op jit(solution)/shard_map/ppermute | solution.py:62
  81.6 37.5 %collective-permute-start.25 = (bf16[1024,256]{1,0:T(8,128)(2,1)S(1)}, bf16[1024,256]{1,0:T(8,128)(2,1)S(1)}, u32[]{:S(2)}, u32[]{:S(2)}) collective-permute-start(bf16[1024,256]{1,0:T(8,128)(2,1)S(1)} %broadcast_select_fusion.3), channel_id=1, source_target_pairs={{2,0},{3,1},{4,6},{5,7},{10,8},{11,9},{12,14},{13,15},{18,16},{19,... | collective-permute-start | bytes 1572872 | tf_op jit(solution)/shard_map/ppermute | solution.py:62
  92.0 6.8 %collective-permute-start.26 = (bf16[1024,256]{1,0:T(8,128)(2,1)S(1)}, bf16[1024,256]{1,0:T(8,128)(2,1)S(1)}, u32[]{:S(2)}, u32[]{:S(2)}) collective-permute-start(bf16[1024,256]{1,0:T(8,128)(2,1)S(1)} %collective-permute-done.24), channel_id=1, source_target_pairs={{2,4},{3,5},{10,12},{11,13},{18,20},{19,21},{26,28},{27,29}} | collective-permute-start | bytes 1572872 | tf_op jit(solution)/shard_map/ppermute | solution.py:62
  94.2 21.6 %collective-permute-start.15 = (bf16[1024,512]{1,0:T(8,128)(2,1)S(1)}, bf16[1024,512]{1,0:T(8,128)(2,1)S(1)}, u32[]{:S(2)}, u32[]{:S(2)}) collective-permute-start(bf16[1024,512]{1,0:T(8,128)(2,1)S(1)} %pad_maximum_fusion.1), channel_id=1, source_target_pairs={{0,1},{1,0},{2,3},{3,2},{4,5},{5,4},{6,7},{7,6},{8,9},{9,8},{10,11... | collective-permute-start | bytes 3145736 | tf_op jit(solution)/shard_map/ppermute | solution.py:62
  94.3 20.1 %collective-permute-start.21 = (bf16[1024,256]{1,0:T(8,128)(2,1)S(1)}, bf16[1024,256]{1,0:T(8,128)(2,1)S(1)}, u32[]{:S(2)}, u32[]{:S(2)}) collective-permute-start(bf16[1024,256]{1,0:T(8,128)(2,1)S(1)} %collective-permute-done.20), channel_id=1, source_target_pairs={{4,6},{5,7},{12,14},{13,15},{20,22},{21,23},{28,30},{29,31}} | collective-permute-start | bytes 1572872 | tf_op jit(solution)/shard_map/ppermute | solution.py:62
  98.2 20.2 %collective-permute-start.9 = (bf16[256,1024]{1,0:T(8,128)(2,1)S(1)}, bf16[256,1024]{1,0:T(8,128)(2,1)S(1)}, u32[]{:S(2)}, u32[]{:S(2)}) collective-permute-start(bf16[256,1024]{1,0:T(8,128)(2,1)S(1)} %slice.75), channel_id=1, source_target_pairs={{0,16},{1,17},{2,18},{3,19},{4,20},{5,21},{6,22},{7,23},{8,24},{9,... | collective-permute-start | bytes 1572872 | tf_op jit(solution)/shard_map/ppermute | solution.py:62
  98.8 25.9 %collective-permute-start.27 = (bf16[1024,256]{1,0:T(8,128)(2,1)S(1)}, bf16[1024,256]{1,0:T(8,128)(2,1)S(1)}, u32[]{:S(2)}, u32[]{:S(2)}) collective-permute-start(bf16[1024,256]{1,0:T(8,128)(2,1)S(1)} %collective-permute-done.26), channel_id=1, source_target_pairs={{4,6},{5,7},{12,14},{13,15},{20,22},{21,23},{28,30},{29,31}} | collective-permute-start | bytes 1572872 | tf_op jit(solution)/shard_map/ppermute | solution.py:62
  118.4 6.6 %collective-permute-start.22 = (bf16[1024,512]{1,0:T(8,128)(2,1)S(1)}, bf16[1024,512]{1,0:T(8,128)(2,1)S(1)}, u32[]{:S(2)}, u32[]{:S(2)}) collective-permute-start(bf16[1024,512]{1,0:T(8,128)(2,1)S(1)} %pad_maximum_fusion.2), channel_id=1, source_target_pairs={{0,1},{1,0},{2,3},{3,2},{4,5},{5,4},{6,7},{7,6},{8,9},{9,8},{10,11... | collective-permute-start | bytes 3145736 | tf_op jit(solution)/shard_map/ppermute | solution.py:62
  118.5 14.3 %collective-permute-start.16 = (bf16[256,1024]{1,0:T(8,128)(2,1)S(1)}, bf16[256,1024]{1,0:T(8,128)(2,1)S(1)}, u32[]{:S(2)}, u32[]{:S(2)}) collective-permute-start(bf16[256,1024]{1,0:T(8,128)(2,1)S(1)} %slice.74), channel_id=1, source_target_pairs={{0,16},{1,17},{2,18},{3,19},{4,20},{5,21},{6,22},{7,23},{8,24},{9,... | collective-permute-start | bytes 1572872 | tf_op jit(solution)/shard_map/ppermute | solution.py:62
  133.0 14.8 %collective-permute-start.23 = (bf16[256,1024]{1,0:T(8,128)(2,1)S(1)}, bf16[256,1024]{1,0:T(8,128)(2,1)S(1)}, u32[]{:S(2)}, u32[]{:S(2)}) collective-permute-start(bf16[256,1024]{1,0:T(8,128)(2,1)S(1)} %slice.73), channel_id=1, source_target_pairs={{0,16},{1,17},{2,18},{3,19},{4,20},{5,21},{6,22},{7,23},{8,24},{9,... | collective-permute-start | bytes 1572872 | tf_op jit(solution)/shard_map/ppermute | solution.py:62
  138.1 20.5 %collective-permute-start.29 = (bf16[256,1024]{1,0:T(8,128)(2,1)S(1)}, bf16[256,1024]{1,0:T(8,128)(2,1)S(1)}, u32[]{:S(2)}, u32[]{:S(2)}) collective-permute-start(bf16[256,1024]{1,0:T(8,128)(2,1)S(1)} %slice.72), channel_id=1, source_target_pairs={{0,16},{1,17},{2,18},{3,19},{4,20},{5,21},{6,22},{7,23},{8,24},{9,... | collective-permute-start | bytes 1572872 | tf_op jit(solution)/shard_map/ppermute | solution.py:62
  (11 other events, 60.1 us)

commit v4 on v3

--- a/solution.py
+++ b/solution.py
@@ -138,8 +138,10 @@
     finish(1)
     finish(2, fars[0], given[1])
     finish(3, fars[1], given[2])
-    sums = [a + b.astype(jnp.float32) for a, b in zip(kept, fars)]
-    return jnp.concatenate(sums, 0) / jnp.float32(4 * rows)
+    total = jnp.zeros((cols, cols), jnp.float32)
+    for (lo, hi), mine, far in zip(cuts, kept, fars):
+        total = lax.dynamic_update_slice(total, (mine + far.astype(jnp.float32)) / jnp.float32(4 * rows), (lo, 0))
+    return total
 
 
 def solution(mesh):

time: 163 us -> 161 us (0.988)
  other arithmetic: 18.7 us -> 16.9 us
    div x1, other arithmetic: 2.86 us -> 0.15 us  [per_device(): (mine + far.astype(jnp.float32)) / jnp.float32(4 * rows)]
  transfers between devices with their start and end apart: 30 -> 30, of which waited for: 12 -> 12; matrix products, arithmetic and copies ran while one was open for 14% -> 15% of each run, Pallas kernels for 0% -> 0%
where the time goes in v4:
time: 161 us; the launch traced here: 160 us
  waiting for transfers between devices  104 us (65%)
  starting transfers between devices  26.3 us (16%)
  other arithmetic  16.9 us (10%)
  matrix products  10.1 us (6%)
  local copies, waits for them, and re-layouts  1.63 us (1%)
    ppermute x30, waiting for transfers between devices, send(): return lax.ppermute(value, ('row', 'col'), perm)  104 us
    ppermute x30, starting transfers between devices, send(): return lax.ppermute(value, ('row', 'col'), perm)  26.3 us
    dot_general x8, matrix products, dot(): lax.dot_general(lhs, rhs, (((0,), (0,)), ((), ())), preferred_element_typ...  10.1 us
    select_n x4, other arithmetic, finish(): jnp.where(y == 1, high, low)  4.56 us
    select_n x2, other arithmetic, keep(): return jnp.where(live, block, jnp.zeros_like(block))  4.33 us
  transfers between devices with their start and end apart: 30, of which 12 were waited for; matrix products, arithmetic and copies ran while one was open for 15% of the time, Pallas kernels for 0%

profile of v4, /device:TPU:30, one launch (start us, length us, event | category | flops | bytes accessed | tf_op | source)
XLA Modules:
  0.0 160.3 jit_solution(862019727622430584)
XLA Ops:
  0.7 2.9 %slice_select_fusion = (bf16[1024,256]{1,0:T(8,128)(2,1)}, bf16[1024,256]{1,0:T(8,128)(2,1)}, bf16[1024,256]{1,0:T(8,128)(2,1)S(1)}, bf16[1024,256]{1,0:T(8,128)(2,1)}) fusion(bf16[1024,1024]{1,0:T(8,128)(2,1)} %param.3, pred[]{:T(512)} %bitcast), kind=kLoop, calls=%fused_computation.32 | loop fusion | flops 1048576 | bytes 4194305 | tf_op jit(solution)/shard_map/jit(_where)/select_n | solution.py:86
  3.5 1.5 collective-permute-start
  5.5 3.1 %collective-permute-done.5 = s32[1024]{0:T(1024)S(1)} collective-permute-done((s32[1024]{0:T(1024)S(1)}, s32[1024]{0:T(1024)S(1)}, u32[]{:S(2)}, u32[]{:S(2)}) %collective-permute-start.5) | collective-permute-done | bytes 4128 | tf_op jit(solution)/shard_map/ppermute | solution.py:62
  8.6 1.5 collective-permute-start.10
  10.1 1.5 collective-permute-start.1
  16.1 1.5 broadcast_select_fusion
  18.1 1.4 collective-permute-start.3
  21.8 15.2 %collective-permute-done.2 = bf16[1024,256]{1,0:T(8,128)(2,1)S(1)} collective-permute-done((bf16[1024,256]{1,0:T(8,128)(2,1)S(1)}, bf16[1024,256]{1,0:T(8,128)(2,1)S(1)}, u32[]{:S(2)}, u32[]{:S(2)}) %collective-permute-start.2) | collective-permute-done | bytes 524320 | tf_op jit(solution)/shard_map/ppermute | solution.py:62
  37.8 1.5 collective-permute-start.18
  40.7 11.8 %collective-permute-done.12 = bf16[1024,256]{1,0:T(8,128)(2,1)} collective-permute-done((bf16[1024,256]{1,0:T(8,128)(2,1)}, bf16[1024,256]{1,0:T(8,128)(2,1)}, u32[]{:S(2)}, u32[]{:S(2)}) %collective-permute-start.12) | collective-permute-done | bytes 524320 | tf_op jit(solution)/shard_map/ppermute | solution.py:62
  55.6 12.1 %collective-permute-done.4 = bf16[1024,256]{1,0:T(8,128)(2,1)} collective-permute-done((bf16[1024,256]{1,0:T(8,128)(2,1)}, bf16[1024,256]{1,0:T(8,128)(2,1)}, u32[]{:S(2)}, u32[]{:S(2)}) %collective-permute-start.4) | collective-permute-done | bytes 524320 | tf_op jit(solution)/shard_map/ppermute | solution.py:62
  68.4 1.8 %broadcast_select_fusion.14 = (bf16[1024,256]{1,0:T(8,128)(2,1)S(1)}, bf16[1024,256]{1,0:T(8,128)(2,1)S(1)}, bf16[1024,256]{1,0:T(8,128)(2,1)S(1)}) fusion(pred[]{:T(512)S(6)} %eq.13, bf16[1024,256]{1,0:T(8,128)(2,1)} %collective-permute-done, bf16[1024,256]{1,0:T(8,128)(2,1)} %collective-permute-done.1, bf16[1024,256]{1,0:T(8,128)(2,1)} %copy-done.4, ...), kind=kLoop, calls=%fused_computation.51 | loop fusion | flops 1572864 | bytes 4194308 | tf_op jit(solution)/shard_map/jit(_where)/select_n | solution.py:112
  71.8 9.0 %collective-permute-done.19 = bf16[1024,256]{1,0:T(8,128)(2,1)S(1)} collective-permute-done((bf16[1024,256]{1,0:T(8,128)(2,1)S(1)}, bf16[1024,256]{1,0:T(8,128)(2,1)S(1)}, u32[]{:S(2)}, u32[]{:S(2)}) %collective-permute-start.19) | collective-permute-done | bytes 524320 | tf_op jit(solution)/shard_map/ppermute | solution.py:62
  81.6 1.4 collective-permute-start.25
  83.1 2.5 %broadcast_select_fusion.2 = (bf16[1024,1024]{1,0:T(8,128)(2,1)S(1)}, bf16[1024,1024]{1,0:T(8,128)(2,1)S(1)}) fusion(pred[]{:T(512)S(6)} %eq.17, f32[1024]{0:T(1024)S(1)} %convert_element_type.36, bf16[1024,1024]{1,0:T(8,128)(2,1)} %collective-permute-done.7, f32[1024]{0:T(1024)S(1)} %convert_element_type.39, bf16[1024,1024]{1,0:T(8,128)(2,1)S(1)} %copy-done, ...), kind=kLoop, calls=%fused_computation.4 | loop fusion | flops 9437184 | bytes 8396802 | tf_op jit(solution)/shard_map/jit(_where)/select_n | solution.py:136
  85.6 6.4 %collective-permute-done.14 = bf16[1024,256]{1,0:T(8,128)(2,1)S(1)} collective-permute-done((bf16[1024,256]{1,0:T(8,128)(2,1)S(1)}, bf16[1024,256]{1,0:T(8,128)(2,1)S(1)}, u32[]{:S(2)}, u32[]{:S(2)}) %collective-permute-start.14) | collective-permute-done | bytes 524320 | tf_op jit(solution)/shard_map/ppermute | solution.py:62
  92.7 1.4 broadcast_select_fusion.12
  98.8 1.5 collective-permute-start.27
  100.3 14.2 %collective-permute-done.21 = bf16[1024,256]{1,0:T(8,128)(2,1)S(1)} collective-permute-done((bf16[1024,256]{1,0:T(8,128)(2,1)S(1)}, bf16[1024,256]{1,0:T(8,128)(2,1)S(1)}, u32[]{:S(2)}, u32[]{:S(2)}) %collective-permute-start.21) | collective-permute-done | bytes 524320 | tf_op jit(solution)/shard_map/ppermute | solution.py:62
  119.1 5.6 %collective-permute-done.27 = bf16[1024,256]{1,0:T(8,128)(2,1)S(1)} collective-permute-done((bf16[1024,256]{1,0:T(8,128)(2,1)S(1)}, bf16[1024,256]{1,0:T(8,128)(2,1)S(1)}, u32[]{:S(2)}, u32[]{:S(2)}) %collective-permute-start.27) | collective-permute-done | bytes 524320 | tf_op jit(solution)/shard_map/ppermute | solution.py:62
  127.7 5.2 %collective-permute-done.16 = bf16[256,1024]{1,0:T(8,128)(2,1)S(1)} collective-permute-done((bf16[256,1024]{1,0:T(8,128)(2,1)S(1)}, bf16[256,1024]{1,0:T(8,128)(2,1)S(1)}, u32[]{:S(2)}, u32[]{:S(2)}) %collective-permute-start.16) | collective-permute-done | bytes 524320 | tf_op jit(solution)/shard_map/ppermute | solution.py:62
  134.1 1.4 collective-permute-done.28
  138.9 9.4 %collective-permute-done.23 = bf16[256,1024]{1,0:T(8,128)(2,1)S(1)} collective-permute-done((bf16[256,1024]{1,0:T(8,128)(2,1)S(1)}, bf16[256,1024]{1,0:T(8,128)(2,1)S(1)}, u32[]{:S(2)}, u32[]{:S(2)}) %collective-permute-start.23) | collective-permute-done | bytes 524320 | tf_op jit(solution)/shard_map/ppermute | solution.py:62
  148.5 10.7 %collective-permute-done.29 = bf16[256,1024]{1,0:T(8,128)(2,1)S(1)} collective-permute-done((bf16[256,1024]{1,0:T(8,128)(2,1)S(1)}, bf16[256,1024]{1,0:T(8,128)(2,1)S(1)}, u32[]{:S(2)}, u32[]{:S(2)}) %collective-permute-start.29) | collective-permute-done | bytes 524320 | tf_op jit(solution)/shard_map/ppermute | solution.py:62
  (86 shorter events, 34.7 us)
Async XLA Ops:
  11.5 10.2 %collective-permute-start.17 = (bf16[1024,256]{1,0:T(8,128)(2,1)}, bf16[1024,256]{1,0:T(8,128)(2,1)S(1)}, u32[]{:S(2)}, u32[]{:S(2)}) collective-permute-start(bf16[1024,256]{1,0:T(8,128)(2,1)} %get-tuple-element.37), channel_id=1, source_target_pairs={{0,0},{1,8},{2,2},{3,10},{8,1},{9,9},{10,3},{11,11},{16,16},{17,24... | collective-permute-start | bytes 1572872 | tf_op jit(solution)/shard_map/ppermute | solution.py:62
  13.0 6.6 %collective-permute-start.11 = (bf16[1024,256]{1,0:T(8,128)(2,1)}, bf16[1024,256]{1,0:T(8,128)(2,1)S(1)}, u32[]{:S(2)}, u32[]{:S(2)}) collective-permute-start(bf16[1024,256]{1,0:T(8,128)(2,1)} %collective-permute-done.10), channel_id=1, source_target_pairs={{0,2},{1,3},{2,4},{3,5},{8,10},{9,11},{10,12},{11,13},{16,18},{17,... | collective-permute-start | bytes 1572872 | tf_op jit(solution)/shard_map/ppermute | solution.py:62
  14.8 22.2 %collective-permute-start.2 = (bf16[1024,256]{1,0:T(8,128)(2,1)S(1)}, bf16[1024,256]{1,0:T(8,128)(2,1)S(1)}, u32[]{:S(2)}, u32[]{:S(2)}) collective-permute-start(bf16[1024,256]{1,0:T(8,128)(2,1)S(1)} %broadcast_select_fusion.6), channel_id=1, source_target_pairs={{2,0},{3,1},{4,6},{5,7},{10,8},{11,9},{12,14},{13,15},{18,16},{19,... | collective-permute-start | bytes 1572872 | tf_op jit(solution)/shard_map/ppermute | solution.py:62
  17.6 65.5 %collective-permute-start.7 = (bf16[1024,1024]{1,0:T(8,128)(2,1)}, bf16[1024,1024]{1,0:T(8,128)(2,1)}, u32[]{:S(2)}, u32[]{:S(2)}) collective-permute-start(bf16[1024,1024]{1,0:T(8,128)(2,1)} %broadcast_select_fusion), channel_id=1, source_target_pairs={{0,8},{1,9},{2,10},{3,11},{4,12},{5,13},{6,14},{7,15},{8,0},{9,1},... | collective-permute-start | bytes 6291464 | tf_op jit(solution)/shard_map/ppermute | solution.py:62
  18.1 21.2 %collective-permute-start.3 = (bf16[1024,256]{1,0:T(8,128)(2,1)}, bf16[1024,256]{1,0:T(8,128)(2,1)}, u32[]{:S(2)}, u32[]{:S(2)}) collective-permute-start(bf16[1024,256]{1,0:T(8,128)(2,1)} %collective-permute-done.1), channel_id=1, source_target_pairs={{2,4},{3,5},{10,12},{11,13},{18,20},{19,21},{26,28},{27,29}} | collective-permute-start | bytes 1572872 | tf_op jit(solution)/shard_map/ppermute | solution.py:62
  20.5 32.1 %collective-permute-start.12 = (bf16[1024,256]{1,0:T(8,128)(2,1)}, bf16[1024,256]{1,0:T(8,128)(2,1)}, u32[]{:S(2)}, u32[]{:S(2)}) collective-permute-start(bf16[1024,256]{1,0:T(8,128)(2,1)} %broadcast_select_fusion.5), channel_id=1, source_target_pairs={{2,0},{3,1},{4,6},{5,7},{10,8},{11,9},{12,14},{13,15},{18,16},{19,... | collective-permute-start | bytes 1572872 | tf_op jit(solution)/shard_map/ppermute | solution.py:62
  37.8 15.4 %collective-permute-start.18 = (bf16[1024,256]{1,0:T(8,128)(2,1)S(1)}, bf16[1024,256]{1,0:T(8,128)(2,1)}, u32[]{:S(2)}, u32[]{:S(2)}) collective-permute-start(bf16[1024,256]{1,0:T(8,128)(2,1)S(1)} %collective-permute-done.17), channel_id=1, source_target_pairs={{0,2},{1,3},{2,4},{3,5},{8,10},{9,11},{10,12},{11,13},{16,18},{17,... | collective-permute-start | bytes 1572872 | tf_op jit(solution)/shard_map/ppermute | solution.py:62
  39.3 28.4 %collective-permute-start.4 = (bf16[1024,256]{1,0:T(8,128)(2,1)}, bf16[1024,256]{1,0:T(8,128)(2,1)}, u32[]{:S(2)}, u32[]{:S(2)}) collective-permute-start(bf16[1024,256]{1,0:T(8,128)(2,1)} %collective-permute-done.3), channel_id=1, source_target_pairs={{4,6},{5,7},{12,14},{13,15},{20,22},{21,23},{28,30},{29,31}} | collective-permute-start | bytes 1572872 | tf_op jit(solution)/shard_map/ppermute | solution.py:62
  52.5 18.0 %collective-permute-start.13 = (bf16[1024,256]{1,0:T(8,128)(2,1)}, bf16[1024,256]{1,0:T(8,128)(2,1)S(1)}, u32[]{:S(2)}, u32[]{:S(2)}) collective-permute-start(bf16[1024,256]{1,0:T(8,128)(2,1)} %copy-done.2), channel_id=1, source_target_pairs={{2,4},{3,5},{10,12},{11,13},{18,20},{19,21},{26,28},{27,29}} | collective-permute-start | bytes 1572872 | tf_op jit(solution)/shard_map/ppermute | solution.py:62
  54.3 26.5 %collective-permute-start.19 = (bf16[1024,256]{1,0:T(8,128)(2,1)S(1)}, bf16[1024,256]{1,0:T(8,128)(2,1)S(1)}, u32[]{:S(2)}, u32[]{:S(2)}) collective-permute-start(bf16[1024,256]{1,0:T(8,128)(2,1)S(1)} %broadcast_select_fusion.4), channel_id=1, source_target_pairs={{2,0},{3,1},{4,6},{5,7},{10,8},{11,9},{12,14},{13,15},{18,16},{19,... | collective-permute-start | bytes 1572872 | tf_op jit(solution)/shard_map/ppermute | solution.py:62
  67.8 13.8 %collective-permute-start.24 = (bf16[1024,256]{1,0:T(8,128)(2,1)S(1)}, bf16[1024,256]{1,0:T(8,128)(2,1)S(1)}, u32[]{:S(2)}, u32[]{:S(2)}) collective-permute-start(bf16[1024,256]{1,0:T(8,128)(2,1)S(1)} %collective-permute-done.6), channel_id=1, source_target_pairs={{0,2},{1,3},{2,4},{3,5},{8,10},{9,11},{10,12},{11,13},{16,18},{17,... | collective-permute-start | bytes 1572872 | tf_op jit(solution)/shard_map/ppermute | solution.py:62
  70.4 25.2 %collective-permute-start.8 = (bf16[1024,512]{1,0:T(8,128)(2,1)S(1)}, bf16[1024,512]{1,0:T(8,128)(2,1)S(1)}, u32[]{:S(2)}, u32[]{:S(2)}) collective-permute-start(bf16[1024,512]{1,0:T(8,128)(2,1)S(1)} %pad_maximum_fusion), channel_id=1, source_target_pairs={{0,1},{1,0},{2,3},{3,2},{4,5},{5,4},{6,7},{7,6},{8,9},{9,8},{10,11... | collective-permute-start | bytes 3145736 | tf_op jit(solution)/shard_map/ppermute | solution.py:62
  70.5 21.4 %collective-permute-start.14 = (bf16[1024,256]{1,0:T(8,128)(2,1)S(1)}, bf16[1024,256]{1,0:T(8,128)(2,1)S(1)}, u32[]{:S(2)}, u32[]{:S(2)}) collective-permute-start(bf16[1024,256]{1,0:T(8,128)(2,1)S(1)} %collective-permute-done.13), channel_id=1, source_target_pairs={{4,6},{5,7},{12,14},{13,15},{20,22},{21,23},{28,30},{29,31}} | collective-permute-start | bytes 1572872 | tf_op jit(solution)/shard_map/ppermute | solution.py:62
  80.8 13.4 %collective-permute-start.20 = (bf16[1024,256]{1,0:T(8,128)(2,1)}, bf16[1024,256]{1,0:T(8,128)(2,1)S(1)}, u32[]{:S(2)}, u32[]{:S(2)}) collective-permute-start(bf16[1024,256]{1,0:T(8,128)(2,1)} %collective-permute-done.18), channel_id=1, source_target_pairs={{2,4},{3,5},{10,12},{11,13},{18,20},{19,21},{26,28},{27,29}} | collective-permute-start | bytes 1572872 | tf_op jit(solution)/shard_map/ppermute | solution.py:62
  81.6 37.5 %collective-permute-start.25 = (bf16[1024,256]{1,0:T(8,128)(2,1)S(1)}, bf16[1024,256]{1,0:T(8,128)(2,1)S(1)}, u32[]{:S(2)}, u32[]{:S(2)}) collective-permute-start(bf16[1024,256]{1,0:T(8,128)(2,1)S(1)} %broadcast_select_fusion.3), channel_id=1, source_target_pairs={{2,0},{3,1},{4,6},{5,7},{10,8},{11,9},{12,14},{13,15},{18,16},{19,... | collective-permute-start | bytes 1572872 | tf_op jit(solution)/shard_map/ppermute | solution.py:62
  92.0 6.8 %collective-permute-start.26 = (bf16[1024,256]{1,0:T(8,128)(2,1)S(1)}, bf16[1024,256]{1,0:T(8,128)(2,1)S(1)}, u32[]{:S(2)}, u32[]{:S(2)}) collective-permute-start(bf16[1024,256]{1,0:T(8,128)(2,1)S(1)} %collective-permute-done.24), channel_id=1, source_target_pairs={{2,4},{3,5},{10,12},{11,13},{18,20},{19,21},{26,28},{27,29}} | collective-permute-start | bytes 1572872 | tf_op jit(solution)/shard_map/ppermute | solution.py:62
  94.2 21.6 %collective-permute-start.15 = (bf16[1024,512]{1,0:T(8,128)(2,1)S(1)}, bf16[1024,512]{1,0:T(8,128)(2,1)S(1)}, u32[]{:S(2)}, u32[]{:S(2)}) collective-permute-start(bf16[1024,512]{1,0:T(8,128)(2,1)S(1)} %pad_maximum_fusion.1), channel_id=1, source_target_pairs={{0,1},{1,0},{2,3},{3,2},{4,5},{5,4},{6,7},{7,6},{8,9},{9,8},{10,11... | collective-permute-start | bytes 3145736 | tf_op jit(solution)/shard_map/ppermute | solution.py:62
  94.3 20.1 %collective-permute-start.21 = (bf16[1024,256]{1,0:T(8,128)(2,1)S(1)}, bf16[1024,256]{1,0:T(8,128)(2,1)S(1)}, u32[]{:S(2)}, u32[]{:S(2)}) collective-permute-start(bf16[1024,256]{1,0:T(8,128)(2,1)S(1)} %collective-permute-done.20), channel_id=1, source_target_pairs={{4,6},{5,7},{12,14},{13,15},{20,22},{21,23},{28,30},{29,31}} | collective-permute-start | bytes 1572872 | tf_op jit(solution)/shard_map/ppermute | solution.py:62
  98.2 20.2 %collective-permute-start.9 = (bf16[256,1024]{1,0:T(8,128)(2,1)S(1)}, bf16[256,1024]{1,0:T(8,128)(2,1)S(1)}, u32[]{:S(2)}, u32[]{:S(2)}) collective-permute-start(bf16[256,1024]{1,0:T(8,128)(2,1)S(1)} %slice.89), channel_id=1, source_target_pairs={{0,16},{1,17},{2,18},{3,19},{4,20},{5,21},{6,22},{7,23},{8,24},{9,... | collective-permute-start | bytes 1572872 | tf_op jit(solution)/shard_map/ppermute | solution.py:62
  98.8 25.9 %collective-permute-start.27 = (bf16[1024,256]{1,0:T(8,128)(2,1)S(1)}, bf16[1024,256]{1,0:T(8,128)(2,1)S(1)}, u32[]{:S(2)}, u32[]{:S(2)}) collective-permute-start(bf16[1024,256]{1,0:T(8,128)(2,1)S(1)} %collective-permute-done.26), channel_id=1, source_target_pairs={{4,6},{5,7},{12,14},{13,15},{20,22},{21,23},{28,30},{29,31}} | collective-permute-start | bytes 1572872 | tf_op jit(solution)/shard_map/ppermute | solution.py:62
  118.4 6.6 %collective-permute-start.22 = (bf16[1024,512]{1,0:T(8,128)(2,1)S(1)}, bf16[1024,512]{1,0:T(8,128)(2,1)S(1)}, u32[]{:S(2)}, u32[]{:S(2)}) collective-permute-start(bf16[1024,512]{1,0:T(8,128)(2,1)S(1)} %pad_maximum_fusion.2), channel_id=1, source_target_pairs={{0,1},{1,0},{2,3},{3,2},{4,5},{5,4},{6,7},{7,6},{8,9},{9,8},{10,11... | collective-permute-start | bytes 3145736 | tf_op jit(solution)/shard_map/ppermute | solution.py:62
  118.5 14.3 %collective-permute-start.16 = (bf16[256,1024]{1,0:T(8,128)(2,1)S(1)}, bf16[256,1024]{1,0:T(8,128)(2,1)S(1)}, u32[]{:S(2)}, u32[]{:S(2)}) collective-permute-start(bf16[256,1024]{1,0:T(8,128)(2,1)S(1)} %slice.88), channel_id=1, source_target_pairs={{0,16},{1,17},{2,18},{3,19},{4,20},{5,21},{6,22},{7,23},{8,24},{9,... | collective-permute-start | bytes 1572872 | tf_op jit(solution)/shard_map/ppermute | solution.py:62
  133.5 14.8 %collective-permute-start.23 = (bf16[256,1024]{1,0:T(8,128)(2,1)S(1)}, bf16[256,1024]{1,0:T(8,128)(2,1)S(1)}, u32[]{:S(2)}, u32[]{:S(2)}) collective-permute-start(bf16[256,1024]{1,0:T(8,128)(2,1)S(1)} %slice.87), channel_id=1, source_target_pairs={{0,16},{1,17},{2,18},{3,19},{4,20},{5,21},{6,22},{7,23},{8,24},{9,... | collective-permute-start | bytes 1572872 | tf_op jit(solution)/shard_map/ppermute | solution.py:62
  138.1 21.0 %collective-permute-start.29 = (bf16[256,1024]{1,0:T(8,128)(2,1)S(1)}, bf16[256,1024]{1,0:T(8,128)(2,1)S(1)}, u32[]{:S(2)}, u32[]{:S(2)}) collective-permute-start(bf16[256,1024]{1,0:T(8,128)(2,1)S(1)} %slice.86), channel_id=1, source_target_pairs={{0,16},{1,17},{2,18},{3,19},{4,20},{5,21},{6,22},{7,23},{8,24},{9,... | collective-permute-start | bytes 1572872 | tf_op jit(solution)/shard_map/ppermute | solution.py:62
  (12 other events, 70.6 us)

commit v5 on v4

--- a/solution.py
+++ b/solution.py
@@ -132,8 +132,9 @@
     out[2, 1] = send(up[2, 1], TWO_TO_THREE)
     up[3, 1] = send(after(up[3, 0], up[1, 1], out[1, 1]), ONE_TO_TWO)
     out[3, 1] = send(up[3, 1], TWO_TO_THREE)
-    here, there = scale(own, playlist_weights), scale(near, w_near)
-    by_mine, by_their = jnp.where(k == x, here, there), jnp.where(k == x, there, here)
+    same = k == x
+    by_mine = scale(jnp.where(same, own, near), jnp.where(same, playlist_weights, w_near))
+    by_their = scale(jnp.where(same, near, own), jnp.where(same, w_near, playlist_weights))
     finish(0)
     finish(1)
     finish(2, fars[0], given[1])

time: 161 us -> 161 us (level)
    convert_element_type x0 -> x1, other arithmetic: none -> 2.68 us  [scale(): (weight[:, None].astype(jnp.float32) * block.astype(jnp.float32)).astype(...]
    select_n x1 -> x0, other arithmetic: 2.54 us -> none  [per_device(): jnp.where(k == x, here, there)]
where the time goes in v5:
time: 161 us; the launch traced here: 160 us
  waiting for transfers between devices  104 us (65%)
  starting transfers between devices  26.2 us (16%)
  other arithmetic  17 us (11%)
  matrix products  10.1 us (6%)
  local copies, waits for them, and re-layouts  1.63 us (1%)
    ppermute x30, waiting for transfers between devices, send(): return lax.ppermute(value, ('row', 'col'), perm)  104 us
    ppermute x30, starting transfers between devices, send(): return lax.ppermute(value, ('row', 'col'), perm)  26.2 us
    dot_general x8, matrix products, dot(): lax.dot_general(lhs, rhs, (((0,), (0,)), ((), ())), preferred_element_typ...  10.1 us
    select_n x4, other arithmetic, finish(): jnp.where(y == 1, high, low)  4.56 us
    select_n x2, other arithmetic, keep(): return jnp.where(live, block, jnp.zeros_like(block))  4.33 us
  transfers between devices with their start and end apart: 30, of which 12 were waited for; matrix products, arithmetic and copies ran while one was open for 15% of the time, Pallas kernels for 0%

profile of v5, /device:TPU:30, one launch (start us, length us, event | category | flops | bytes accessed | tf_op | source)
XLA Modules:
  0.0 160.5 jit_solution(2796632707631265690)
XLA Ops:
  0.7 2.9 %slice_select_fusion = (bf16[1024,256]{1,0:T(8,128)(2,1)}, bf16[1024,256]{1,0:T(8,128)(2,1)}, bf16[1024,256]{1,0:T(8,128)(2,1)S(1)}, bf16[1024,256]{1,0:T(8,128)(2,1)}) fusion(bf16[1024,1024]{1,0:T(8,128)(2,1)} %param.3, pred[]{:T(512)} %bitcast), kind=kLoop, calls=%fused_computation.30 | loop fusion | flops 1048576 | bytes 4194305 | tf_op jit(solution)/shard_map/jit(_where)/select_n | solution.py:86
  3.5 1.5 collective-permute-start
  5.5 3.1 %collective-permute-done.5 = s32[1024]{0:T(1024)S(1)} collective-permute-done((s32[1024]{0:T(1024)S(1)}, s32[1024]{0:T(1024)S(1)}, u32[]{:S(2)}, u32[]{:S(2)}) %collective-permute-start.5) | collective-permute-done | bytes 4128 | tf_op jit(solution)/shard_map/ppermute | solution.py:62
  8.6 1.5 collective-permute-start.10
  10.1 1.5 collective-permute-start.1
  14.8 1.3 collective-permute-start.2
  16.1 1.5 broadcast_select_fusion
  18.1 1.5 collective-permute-start.3
  21.8 15.2 %collective-permute-done.2 = bf16[1024,256]{1,0:T(8,128)(2,1)S(1)} collective-permute-done((bf16[1024,256]{1,0:T(8,128)(2,1)S(1)}, bf16[1024,256]{1,0:T(8,128)(2,1)S(1)}, u32[]{:S(2)}, u32[]{:S(2)}) %collective-permute-start.2) | collective-permute-done | bytes 524320 | tf_op jit(solution)/shard_map/ppermute | solution.py:62
  37.8 1.5 collective-permute-start.18
  40.7 11.9 %collective-permute-done.12 = bf16[1024,256]{1,0:T(8,128)(2,1)} collective-permute-done((bf16[1024,256]{1,0:T(8,128)(2,1)}, bf16[1024,256]{1,0:T(8,128)(2,1)}, u32[]{:S(2)}, u32[]{:S(2)}) %collective-permute-start.12) | collective-permute-done | bytes 524320 | tf_op jit(solution)/shard_map/ppermute | solution.py:62
  55.7 12.1 %collective-permute-done.4 = bf16[1024,256]{1,0:T(8,128)(2,1)} collective-permute-done((bf16[1024,256]{1,0:T(8,128)(2,1)}, bf16[1024,256]{1,0:T(8,128)(2,1)}, u32[]{:S(2)}, u32[]{:S(2)}) %collective-permute-start.4) | collective-permute-done | bytes 524320 | tf_op jit(solution)/shard_map/ppermute | solution.py:62
  68.4 1.8 %broadcast_select_fusion.12 = (bf16[1024,256]{1,0:T(8,128)(2,1)S(1)}, bf16[1024,256]{1,0:T(8,128)(2,1)S(1)}, bf16[1024,256]{1,0:T(8,128)(2,1)S(1)}) fusion(pred[]{:T(512)S(6)} %eq.13, bf16[1024,256]{1,0:T(8,128)(2,1)} %collective-permute-done, bf16[1024,256]{1,0:T(8,128)(2,1)} %collective-permute-done.1, bf16[1024,256]{1,0:T(8,128)(2,1)} %copy-done.4, ...), kind=kLoop, calls=%fused_computation.49 | loop fusion | flops 1572864 | bytes 4194308 | tf_op jit(solution)/shard_map/jit(_where)/select_n | solution.py:112
  71.8 9.0 %collective-permute-done.19 = bf16[1024,256]{1,0:T(8,128)(2,1)S(1)} collective-permute-done((bf16[1024,256]{1,0:T(8,128)(2,1)S(1)}, bf16[1024,256]{1,0:T(8,128)(2,1)S(1)}, u32[]{:S(2)}, u32[]{:S(2)}) %collective-permute-start.19) | collective-permute-done | bytes 524320 | tf_op jit(solution)/shard_map/ppermute | solution.py:62
  82.9 2.7 %multiply_convert_fusion.1 = (bf16[1024,1024]{1,0:T(8,128)(2,1)S(1)}, bf16[1024,1024]{1,0:T(8,128)(2,1)S(1)}) fusion(bf16[1024,1024]{1,0:T(8,128)(2,1)} %collective-permute-done.7, f32[1024]{0:T(1024)S(1)} %get-tuple-element.41, pred[]{:T(512)S(6)} %eq.17, f32[1024]{0:T(1024)S(1)} %get-tuple-element.42, bf16[1024,1024]{1,0:T(8,128)(2,1)S(1)} %copy-done, pred[]{:T(512)} %bitcast), kind=kLoop, calls=%fused_computation.1 | loop fusion | flops 9437184 | bytes 8396802 | tf_op jit(solution)/shard_map/convert_element_type | solution.py:101
  85.6 6.5 %collective-permute-done.14 = bf16[1024,256]{1,0:T(8,128)(2,1)S(1)} collective-permute-done((bf16[1024,256]{1,0:T(8,128)(2,1)S(1)}, bf16[1024,256]{1,0:T(8,128)(2,1)S(1)}, u32[]{:S(2)}, u32[]{:S(2)}) %collective-permute-start.14) | collective-permute-done | bytes 524320 | tf_op jit(solution)/shard_map/ppermute | solution.py:62
  92.8 1.4 broadcast_select_fusion.10
  98.9 1.5 collective-permute-start.27
  100.4 14.2 %collective-permute-done.21 = bf16[1024,256]{1,0:T(8,128)(2,1)S(1)} collective-permute-done((bf16[1024,256]{1,0:T(8,128)(2,1)S(1)}, bf16[1024,256]{1,0:T(8,128)(2,1)S(1)}, u32[]{:S(2)}, u32[]{:S(2)}) %collective-permute-start.21) | collective-permute-done | bytes 524320 | tf_op jit(solution)/shard_map/ppermute | solution.py:62
  119.2 5.5 %collective-permute-done.27 = bf16[1024,256]{1,0:T(8,128)(2,1)S(1)} collective-permute-done((bf16[1024,256]{1,0:T(8,128)(2,1)S(1)}, bf16[1024,256]{1,0:T(8,128)(2,1)S(1)}, u32[]{:S(2)}, u32[]{:S(2)}) %collective-permute-start.27) | collective-permute-done | bytes 524320 | tf_op jit(solution)/shard_map/ppermute | solution.py:62
  127.7 5.3 %collective-permute-done.16 = bf16[256,1024]{1,0:T(8,128)(2,1)S(1)} collective-permute-done((bf16[256,1024]{1,0:T(8,128)(2,1)S(1)}, bf16[256,1024]{1,0:T(8,128)(2,1)S(1)}, u32[]{:S(2)}, u32[]{:S(2)}) %collective-permute-start.16) | collective-permute-done | bytes 524320 | tf_op jit(solution)/shard_map/ppermute | solution.py:62
  134.2 1.4 collective-permute-done.28
  139.0 9.4 %collective-permute-done.23 = bf16[256,1024]{1,0:T(8,128)(2,1)S(1)} collective-permute-done((bf16[256,1024]{1,0:T(8,128)(2,1)S(1)}, bf16[256,1024]{1,0:T(8,128)(2,1)S(1)}, u32[]{:S(2)}, u32[]{:S(2)}) %collective-permute-start.23) | collective-permute-done | bytes 524320 | tf_op jit(solution)/shard_map/ppermute | solution.py:62
  148.6 10.7 %collective-permute-done.29 = bf16[256,1024]{1,0:T(8,128)(2,1)S(1)} collective-permute-done((bf16[256,1024]{1,0:T(8,128)(2,1)S(1)}, bf16[256,1024]{1,0:T(8,128)(2,1)S(1)}, u32[]{:S(2)}, u32[]{:S(2)}) %collective-permute-start.29) | collective-permute-done | bytes 524320 | tf_op jit(solution)/shard_map/ppermute | solution.py:62
  (85 shorter events, 34.7 us)
Async XLA Ops:
  3.5 6.5 %collective-permute-start = (bf16[1024,256]{1,0:T(8,128)(2,1)S(1)}, bf16[1024,256]{1,0:T(8,128)(2,1)}, u32[]{:S(2)}, u32[]{:S(2)}) collective-permute-start(bf16[1024,256]{1,0:T(8,128)(2,1)S(1)} %get-tuple-element.39), channel_id=1, source_target_pairs={{0,0},{1,8},{2,2},{3,10},{8,1},{9,9},{10,3},{11,11},{16,16},{17,24... | collective-permute-start | bytes 1572872 | tf_op jit(solution)/shard_map/ppermute | solution.py:62
  11.5 10.2 %collective-permute-start.17 = (bf16[1024,256]{1,0:T(8,128)(2,1)}, bf16[1024,256]{1,0:T(8,128)(2,1)S(1)}, u32[]{:S(2)}, u32[]{:S(2)}) collective-permute-start(bf16[1024,256]{1,0:T(8,128)(2,1)} %get-tuple-element.37), channel_id=1, source_target_pairs={{0,0},{1,8},{2,2},{3,10},{8,1},{9,9},{10,3},{11,11},{16,16},{17,24... | collective-permute-start | bytes 1572872 | tf_op jit(solution)/shard_map/ppermute | solution.py:62
  13.0 6.6 %collective-permute-start.11 = (bf16[1024,256]{1,0:T(8,128)(2,1)}, bf16[1024,256]{1,0:T(8,128)(2,1)S(1)}, u32[]{:S(2)}, u32[]{:S(2)}) collective-permute-start(bf16[1024,256]{1,0:T(8,128)(2,1)} %collective-permute-done.10), channel_id=1, source_target_pairs={{0,2},{1,3},{2,4},{3,5},{8,10},{9,11},{10,12},{11,13},{16,18},{17,... | collective-permute-start | bytes 1572872 | tf_op jit(solution)/shard_map/ppermute | solution.py:62
  14.8 22.2 %collective-permute-start.2 = (bf16[1024,256]{1,0:T(8,128)(2,1)S(1)}, bf16[1024,256]{1,0:T(8,128)(2,1)S(1)}, u32[]{:S(2)}, u32[]{:S(2)}) collective-permute-start(bf16[1024,256]{1,0:T(8,128)(2,1)S(1)} %broadcast_select_fusion.4), channel_id=1, source_target_pairs={{2,0},{3,1},{4,6},{5,7},{10,8},{11,9},{12,14},{13,15},{18,16},{19,... | collective-permute-start | bytes 1572872 | tf_op jit(solution)/shard_map/ppermute | solution.py:62
  17.6 65.4 %collective-permute-start.7 = (bf16[1024,1024]{1,0:T(8,128)(2,1)}, bf16[1024,1024]{1,0:T(8,128)(2,1)}, u32[]{:S(2)}, u32[]{:S(2)}) collective-permute-start(bf16[1024,1024]{1,0:T(8,128)(2,1)} %broadcast_select_fusion), channel_id=1, source_target_pairs={{0,8},{1,9},{2,10},{3,11},{4,12},{5,13},{6,14},{7,15},{8,0},{9,1},... | collective-permute-start | bytes 6291464 | tf_op jit(solution)/shard_map/ppermute | solution.py:62
  18.1 21.2 %collective-permute-start.3 = (bf16[1024,256]{1,0:T(8,128)(2,1)}, bf16[1024,256]{1,0:T(8,128)(2,1)}, u32[]{:S(2)}, u32[]{:S(2)}) collective-permute-start(bf16[1024,256]{1,0:T(8,128)(2,1)} %collective-permute-done.1), channel_id=1, source_target_pairs={{2,4},{3,5},{10,12},{11,13},{18,20},{19,21},{26,28},{27,29}} | collective-permute-start | bytes 1572872 | tf_op jit(solution)/shard_map/ppermute | solution.py:62
  20.5 32.1 %collective-permute-start.12 = (bf16[1024,256]{1,0:T(8,128)(2,1)}, bf16[1024,256]{1,0:T(8,128)(2,1)}, u32[]{:S(2)}, u32[]{:S(2)}) collective-permute-start(bf16[1024,256]{1,0:T(8,128)(2,1)} %broadcast_select_fusion.3), channel_id=1, source_target_pairs={{2,0},{3,1},{4,6},{5,7},{10,8},{11,9},{12,14},{13,15},{18,16},{19,... | collective-permute-start | bytes 1572872 | tf_op jit(solution)/shard_map/ppermute | solution.py:62
  37.8 15.4 %collective-permute-start.18 = (bf16[1024,256]{1,0:T(8,128)(2,1)S(1)}, bf16[1024,256]{1,0:T(8,128)(2,1)}, u32[]{:S(2)}, u32[]{:S(2)}) collective-permute-start(bf16[1024,256]{1,0:T(8,128)(2,1)S(1)} %collective-permute-done.17), channel_id=1, source_target_pairs={{0,2},{1,3},{2,4},{3,5},{8,10},{9,11},{10,12},{11,13},{16,18},{17,... | collective-permute-start | bytes 1572872 | tf_op jit(solution)/shard_map/ppermute | solution.py:62
  39.3 28.4 %collective-permute-start.4 = (bf16[1024,256]{1,0:T(8,128)(2,1)}, bf16[1024,256]{1,0:T(8,128)(2,1)}, u32[]{:S(2)}, u32[]{:S(2)}) collective-permute-start(bf16[1024,256]{1,0:T(8,128)(2,1)} %collective-permute-done.3), channel_id=1, source_target_pairs={{4,6},{5,7},{12,14},{13,15},{20,22},{21,23},{28,30},{29,31}} | collective-permute-start | bytes 1572872 | tf_op jit(solution)/shard_map/ppermute | solution.py:62
  52.5 18.0 %collective-permute-start.13 = (bf16[1024,256]{1,0:T(8,128)(2,1)}, bf16[1024,256]{1,0:T(8,128)(2,1)S(1)}, u32[]{:S(2)}, u32[]{:S(2)}) collective-permute-start(bf16[1024,256]{1,0:T(8,128)(2,1)} %copy-done.2), channel_id=1, source_target_pairs={{2,4},{3,5},{10,12},{11,13},{18,20},{19,21},{26,28},{27,29}} | collective-permute-start | bytes 1572872 | tf_op jit(solution)/shard_map/ppermute | solution.py:62
  54.4 26.5 %collective-permute-start.19 = (bf16[1024,256]{1,0:T(8,128)(2,1)S(1)}, bf16[1024,256]{1,0:T(8,128)(2,1)S(1)}, u32[]{:S(2)}, u32[]{:S(2)}) collective-permute-start(bf16[1024,256]{1,0:T(8,128)(2,1)S(1)} %broadcast_select_fusion.2), channel_id=1, source_target_pairs={{2,0},{3,1},{4,6},{5,7},{10,8},{11,9},{12,14},{13,15},{18,16},{19,... | collective-permute-start | bytes 1572872 | tf_op jit(solution)/shard_map/ppermute | solution.py:62
  67.8 13.8 %collective-permute-start.24 = (bf16[1024,256]{1,0:T(8,128)(2,1)S(1)}, bf16[1024,256]{1,0:T(8,128)(2,1)S(1)}, u32[]{:S(2)}, u32[]{:S(2)}) collective-permute-start(bf16[1024,256]{1,0:T(8,128)(2,1)S(1)} %collective-permute-done.6), channel_id=1, source_target_pairs={{0,2},{1,3},{2,4},{3,5},{8,10},{9,11},{10,12},{11,13},{16,18},{17,... | collective-permute-start | bytes 1572872 | tf_op jit(solution)/shard_map/ppermute | solution.py:62
  70.4 25.3 %collective-permute-start.8 = (bf16[1024,512]{1,0:T(8,128)(2,1)S(1)}, bf16[1024,512]{1,0:T(8,128)(2,1)S(1)}, u32[]{:S(2)}, u32[]{:S(2)}) collective-permute-start(bf16[1024,512]{1,0:T(8,128)(2,1)S(1)} %pad_maximum_fusion), channel_id=1, source_target_pairs={{0,1},{1,0},{2,3},{3,2},{4,5},{5,4},{6,7},{7,6},{8,9},{9,8},{10,11... | collective-permute-start | bytes 3145736 | tf_op jit(solution)/shard_map/ppermute | solution.py:62
  70.5 21.6 %collective-permute-start.14 = (bf16[1024,256]{1,0:T(8,128)(2,1)S(1)}, bf16[1024,256]{1,0:T(8,128)(2,1)S(1)}, u32[]{:S(2)}, u32[]{:S(2)}) collective-permute-start(bf16[1024,256]{1,0:T(8,128)(2,1)S(1)} %collective-permute-done.13), channel_id=1, source_target_pairs={{4,6},{5,7},{12,14},{13,15},{20,22},{21,23},{28,30},{29,31}} | collective-permute-start | bytes 1572872 | tf_op jit(solution)/shard_map/ppermute | solution.py:62
  80.8 13.6 %collective-permute-start.20 = (bf16[1024,256]{1,0:T(8,128)(2,1)}, bf16[1024,256]{1,0:T(8,128)(2,1)S(1)}, u32[]{:S(2)}, u32[]{:S(2)}) collective-permute-start(bf16[1024,256]{1,0:T(8,128)(2,1)} %collective-permute-done.18), channel_id=1, source_target_pairs={{2,4},{3,5},{10,12},{11,13},{18,20},{19,21},{26,28},{27,29}} | collective-permute-start | bytes 1572872 | tf_op jit(solution)/shard_map/ppermute | solution.py:62
  81.6 37.6 %collective-permute-start.25 = (bf16[1024,256]{1,0:T(8,128)(2,1)S(1)}, bf16[1024,256]{1,0:T(8,128)(2,1)S(1)}, u32[]{:S(2)}, u32[]{:S(2)}) collective-permute-start(bf16[1024,256]{1,0:T(8,128)(2,1)S(1)} %broadcast_select_fusion.1), channel_id=1, source_target_pairs={{2,0},{3,1},{4,6},{5,7},{10,8},{11,9},{12,14},{13,15},{18,16},{19,... | collective-permute-start | bytes 1572872 | tf_op jit(solution)/shard_map/ppermute | solution.py:62
  92.1 6.8 %collective-permute-start.26 = (bf16[1024,256]{1,0:T(8,128)(2,1)S(1)}, bf16[1024,256]{1,0:T(8,128)(2,1)S(1)}, u32[]{:S(2)}, u32[]{:S(2)}) collective-permute-start(bf16[1024,256]{1,0:T(8,128)(2,1)S(1)} %collective-permute-done.24), channel_id=1, source_target_pairs={{2,4},{3,5},{10,12},{11,13},{18,20},{19,21},{26,28},{27,29}} | collective-permute-start | bytes 1572872 | tf_op jit(solution)/shard_map/ppermute | solution.py:62
  94.3 21.6 %collective-permute-start.15 = (bf16[1024,512]{1,0:T(8,128)(2,1)S(1)}, bf16[1024,512]{1,0:T(8,128)(2,1)S(1)}, u32[]{:S(2)}, u32[]{:S(2)}) collective-permute-start(bf16[1024,512]{1,0:T(8,128)(2,1)S(1)} %pad_maximum_fusion.1), channel_id=1, source_target_pairs={{0,1},{1,0},{2,3},{3,2},{4,5},{5,4},{6,7},{7,6},{8,9},{9,8},{10,11... | collective-permute-start | bytes 3145736 | tf_op jit(solution)/shard_map/ppermute | solution.py:62
  94.4 20.1 %collective-permute-start.21 = (bf16[1024,256]{1,0:T(8,128)(2,1)S(1)}, bf16[1024,256]{1,0:T(8,128)(2,1)S(1)}, u32[]{:S(2)}, u32[]{:S(2)}) collective-permute-start(bf16[1024,256]{1,0:T(8,128)(2,1)S(1)} %collective-permute-done.20), channel_id=1, source_target_pairs={{4,6},{5,7},{12,14},{13,15},{20,22},{21,23},{28,30},{29,31}} | collective-permute-start | bytes 1572872 | tf_op jit(solution)/shard_map/ppermute | solution.py:62
  98.3 20.2 %collective-permute-start.9 = (bf16[256,1024]{1,0:T(8,128)(2,1)S(1)}, bf16[256,1024]{1,0:T(8,128)(2,1)S(1)}, u32[]{:S(2)}, u32[]{:S(2)}) collective-permute-start(bf16[256,1024]{1,0:T(8,128)(2,1)S(1)} %slice.89), channel_id=1, source_target_pairs={{0,16},{1,17},{2,18},{3,19},{4,20},{5,21},{6,22},{7,23},{8,24},{9,... | collective-permute-start | bytes 1572872 | tf_op jit(solution)/shard_map/ppermute | solution.py:62
  98.9 25.8 %collective-permute-start.27 = (bf16[1024,256]{1,0:T(8,128)(2,1)S(1)}, bf16[1024,256]{1,0:T(8,128)(2,1)S(1)}, u32[]{:S(2)}, u32[]{:S(2)}) collective-permute-start(bf16[1024,256]{1,0:T(8,128)(2,1)S(1)} %collective-permute-done.26), channel_id=1, source_target_pairs={{4,6},{5,7},{12,14},{13,15},{20,22},{21,23},{28,30},{29,31}} | collective-permute-start | bytes 1572872 | tf_op jit(solution)/shard_map/ppermute | solution.py:62
  118.6 14.3 %collective-permute-start.16 = (bf16[256,1024]{1,0:T(8,128)(2,1)S(1)}, bf16[256,1024]{1,0:T(8,128)(2,1)S(1)}, u32[]{:S(2)}, u32[]{:S(2)}) collective-permute-start(bf16[256,1024]{1,0:T(8,128)(2,1)S(1)} %slice.88), channel_id=1, source_target_pairs={{0,16},{1,17},{2,18},{3,19},{4,20},{5,21},{6,22},{7,23},{8,24},{9,... | collective-permute-start | bytes 1572872 | tf_op jit(solution)/shard_map/ppermute | solution.py:62
  133.7 14.8 %collective-permute-start.23 = (bf16[256,1024]{1,0:T(8,128)(2,1)S(1)}, bf16[256,1024]{1,0:T(8,128)(2,1)S(1)}, u32[]{:S(2)}, u32[]{:S(2)}) collective-permute-start(bf16[256,1024]{1,0:T(8,128)(2,1)S(1)} %slice.87), channel_id=1, source_target_pairs={{0,16},{1,17},{2,18},{3,19},{4,20},{5,21},{6,22},{7,23},{8,24},{9,... | collective-permute-start | bytes 1572872 | tf_op jit(solution)/shard_map/ppermute | solution.py:62
  138.2 21.0 %collective-permute-start.29 = (bf16[256,1024]{1,0:T(8,128)(2,1)S(1)}, bf16[256,1024]{1,0:T(8,128)(2,1)S(1)}, u32[]{:S(2)}, u32[]{:S(2)}) collective-permute-start(bf16[256,1024]{1,0:T(8,128)(2,1)S(1)} %slice.86), channel_id=1, source_target_pairs={{0,16},{1,17},{2,18},{3,19},{4,20},{5,21},{6,22},{7,23},{8,24},{9,... | collective-permute-start | bytes 1572872 | tf_op jit(solution)/shard_map/ppermute | solution.py:62
  (12 other events, 69.3 us)
